TPU v7x, 32 devices: a whole 2x2x4 slice. The times are simulated.
32 devices in a mesh: dp: 8 (over z, x), tensor: 4 (over y, core).
Axes of the slice: x: 2, y: 2, z: 4, core: 2. Of those that a mesh axis runs over, the one named last changes fastest.
Arguments:
- tokens: bfloat16 [37824, 768], P(('dp', 'tensor')), may hold values from -6 to 6
- qkv_weight: bfloat16 [3, 768, 768], P(None, 'dp', 'tensor'), may hold values from -0.21875 to 0.21875
- out_weight: bfloat16 [768, 768], P('tensor', 'dp'), may hold values from -1.75 to 1.75
- router: bfloat16 [768, 8], P('tensor', 'dp'), may hold values from -0.109375 to 0.109375
- norm_params: bfloat16 [4, 768], P('tensor', 'dp'), may hold values from -1 to 1.5, as said below
- expert_in: bfloat16 [8, 768, 3072], P('dp', None, 'tensor'), may hold values from -2 to 2
- expert_out: bfloat16 [8, 3072, 768], P('dp', 'tensor'), may hold values from -1.75 to 1.75
- cotangent: bfloat16 [37824, 768], P(('dp', 'tensor')), may hold values from -6 to 6
Outputs:
- output: bfloat16 [37824, 768], P(('dp', 'tensor'))
- input_grad: float32 [37824, 768], P(('dp', 'tensor'))
- qkv_grad: float32 [3, 768, 768], P(None, 'dp', 'tensor')
- out_grad: float32 [768, 768], P('tensor', 'dp')
- router_grad: float32 [768, 8], P('tensor', 'dp')
- norm_grad: float32 [4, 768], P('tensor', 'dp')
- expert_in_grad: float32 [8, 768, 3072], P('dp', None, 'tensor')
- expert_out_grad: float32 [8, 3072, 768], P('dp', 'tensor')
Inputs may be any that keep to these rules, and one draw needn't show every extreme that they name: `norm_params`: rows 0 and 2 are gains, rows 1 and 3 biases.
All inputs are finite; a program needn't handle non-finite values.
Results may differ from a plain program's by a relative error of at most 0.025.
Values may be sent and summed in bfloat16 or wider, within the bound.
No kernel may reach another device: no remote copies, remote signals or barrier semaphores. Data moves between devices by JAX's collectives and lax.ppermute only.
A program may use at most 128 MiB of HBM per device.

v0:
```python
import jax
import jax.numpy as jnp
from jax import lax
from jax.sharding import PartitionSpec as P

HEAD_DIM = 64
SEQ = 197


def layer_stats(values):
    centre = jnp.mean(values, axis=-1, keepdims=True)
    centred = values - centre
    spread = jnp.mean(centred * centred, axis=-1, keepdims=True)
    inv_std = lax.rsqrt(spread + 1e-06)
    return (centred * inv_std, inv_std)


def norm_back(gradient, unit_rows, inv_std, gain_row):
    scaled = gradient * gain_row
    mean_one = jnp.mean(scaled, axis=-1, keepdims=True)
    mean_two = jnp.mean(scaled * unit_rows, axis=-1, keepdims=True)
    return inv_std * (scaled - mean_one - unit_rows * mean_two)


def softmax_over(values, axis_index):
    highest = jnp.max(values, axis=axis_index, keepdims=True)
    scaled = jnp.exp(values - highest)
    return scaled / jnp.sum(scaled, axis=axis_index, keepdims=True)


def block_images(image_count, length):
    wanted = -(-512 // length)
    for candidate in range(1, image_count + 1):
        if image_count % candidate == 0 and candidate >= wanted:
            return candidate
    return image_count


def attend_forward(queries, keys_block, values_block, scale):
    scores = (
        jnp.einsum("iqhc,ikhc->ihqk", queries, keys_block, preferred_element_type=jnp.float32)
        * scale
    )
    highest = jnp.max(scores, axis=-1, keepdims=True)
    scaled = jnp.exp(scores - highest)
    totals = jnp.sum(scaled, axis=-1, keepdims=True)
    weights = (scaled / totals).astype(jnp.bfloat16)
    mixed_heads = jnp.einsum(
        "ihqk,ikhc->iqhc", weights, values_block, preferred_element_type=jnp.float32
    )
    return (mixed_heads.astype(jnp.bfloat16), highest + jnp.log(totals))


def attend_backward(queries, keys_block, values_block, grad_heads, log_totals, scale):
    scores = (
        jnp.einsum("iqhc,ikhc->ihqk", queries, keys_block, preferred_element_type=jnp.float32)
        * scale
    )
    weights = jnp.exp(scores - log_totals)
    grad_values = jnp.einsum(
        "ihqk,iqhc->ikhc",
        weights.astype(jnp.bfloat16),
        grad_heads,
        preferred_element_type=jnp.float32,
    )
    grad_weights = jnp.einsum(
        "iqhc,ikhc->ihqk", grad_heads, values_block, preferred_element_type=jnp.float32
    )
    inner = jnp.sum(weights * grad_weights, axis=-1, keepdims=True)
    grad_scores = (weights * (grad_weights - inner)).astype(jnp.bfloat16)
    grad_queries = scale * jnp.einsum(
        "ihqk,ikhc->iqhc", grad_scores, keys_block, preferred_element_type=jnp.float32
    )
    grad_keys = scale * jnp.einsum(
        "ihqk,iqhc->ikhc", grad_scores, queries, preferred_element_type=jnp.float32
    )
    return (
        grad_queries.astype(jnp.bfloat16),
        grad_keys.astype(jnp.bfloat16),
        grad_values.astype(jnp.bfloat16),
    )


def attention_forward(normed_one, qkv_use, out_use, scale):
    row_count = normed_one.shape[0]
    columns = qkv_use.shape[2]
    head_count = columns // HEAD_DIM
    image_count = row_count // SEQ
    per_step = block_images(image_count, SEQ)
    projected = jnp.einsum(
        "rd,kdc->krc", normed_one, qkv_use, preferred_element_type=jnp.float32
    ).astype(jnp.bfloat16)
    shaped = projected.reshape(3, image_count // per_step, per_step, SEQ, head_count, HEAD_DIM)
    mixed_heads, log_totals = lax.map(
        lambda pieces: attend_forward(pieces[0], pieces[1], pieces[2], scale),
        (shaped[0], shaped[1], shaped[2]),
    )
    mixed_heads = mixed_heads.reshape(row_count, columns)
    partial_out = jnp.dot(mixed_heads, out_use, preferred_element_type=jnp.float32)
    return (partial_out, shaped, mixed_heads, log_totals)


def attention_backward(shaped, grad_mixed, log_totals, scale):
    grad_shaped = grad_mixed.reshape(shaped.shape[1:])
    grad_parts = lax.map(
        lambda pieces: attend_backward(
            pieces[0], pieces[1], pieces[2], pieces[3], pieces[4], scale
        ),
        (shaped[0], shaped[1], shaped[2], grad_shaped, log_totals),
    )
    stacked = jnp.stack(grad_parts)
    row_count = grad_mixed.shape[0]
    return stacked.reshape(3, row_count, grad_mixed.shape[1])


def on_device(
    tokens, qkv_weight, out_weight, router, norm_params, expert_in, expert_out, cotangent
):
    scale = HEAD_DIM ** (-0.5)
    own_rows, width = tokens.shape
    qkv_part, out_part, router_part, norm_part = (
        lax.all_gather(qkv_weight, "dp", axis=1, tiled=True),
        lax.all_gather(out_weight, "dp", axis=1, tiled=True),
        lax.all_gather(router, "dp", axis=1, tiled=True),
        lax.all_gather(norm_params, "dp", axis=1, tiled=True),
    )
    x_rows, router_full, norm_full = (
        lax.all_gather(tokens, "tensor", axis=0, tiled=True),
        lax.all_gather(router_part, "tensor", axis=0, tiled=True),
        lax.all_gather(norm_part, "tensor", axis=0, tiled=True),
    )
    qkv_use, out_use = (qkv_part, out_part)
    norms = norm_full.astype(jnp.float32)
    unit_one, inv_one = layer_stats(x_rows.astype(jnp.float32))
    normed_one = (unit_one * norms[0] + norms[1]).astype(jnp.bfloat16)
    partial_out, shaped, mixed_heads, log_totals = attention_forward(
        normed_one, qkv_use, out_use, scale
    )
    attn_own = lax.psum_scatter(
        partial_out.astype(jnp.bfloat16), "tensor", scatter_dimension=0, tiled=True
    ).astype(jnp.float32)
    residual = tokens.astype(jnp.float32) + attn_own
    unit_two, inv_two = layer_stats(residual)
    normed_two = (unit_two * norms[2] + norms[3]).astype(jnp.bfloat16)
    images = own_rows // SEQ
    experts = router_full.shape[1]
    logits = jnp.dot(normed_two, router_full, preferred_element_type=jnp.float32).reshape(
        images, SEQ, experts
    )
    dispatch = softmax_over(logits, 1)
    combine = softmax_over(logits, 2)
    dispatch_low = dispatch.astype(jnp.bfloat16)
    combine_low = combine.astype(jnp.bfloat16)
    normed_img = normed_two.reshape(images, SEQ, width)
    slot_inputs = jnp.einsum(
        "ise,isd->eid", dispatch_low, normed_img, preferred_element_type=jnp.float32
    ).astype(jnp.bfloat16)
    arrived = lax.all_to_all(slot_inputs, "dp", split_axis=0, concat_axis=1, tiled=True)
    slot_rows = lax.all_gather(arrived, "tensor", axis=1, tiled=True).reshape(-1, width)
    first_weight = expert_in[0]
    second_weight = expert_out[0]
    pre_act = jnp.dot(slot_rows, first_weight, preferred_element_type=jnp.float32)
    hidden = jax.nn.gelu(pre_act, approximate=False).astype(jnp.bfloat16)
    expert_terms = jnp.dot(hidden, second_weight, preferred_element_type=jnp.float32)
    expert_rows = lax.psum_scatter(
        expert_terms.astype(jnp.bfloat16), "tensor", scatter_dimension=0, tiled=True
    )
    returned = lax.all_to_all(
        expert_rows.reshape(-1, images, width), "dp", split_axis=0, concat_axis=1, tiled=True
    ).reshape(experts, images, width)
    mixture = jnp.einsum("ise,eid->isd", combine_low, returned, preferred_element_type=jnp.float32)
    output = (residual + mixture.reshape(own_rows, width)).astype(jnp.bfloat16)
    grad_output = cotangent.astype(jnp.float32)
    grad_img = cotangent.reshape(images, SEQ, width)
    grad_combine = jnp.einsum(
        "isd,eid->ise", grad_img, returned, preferred_element_type=jnp.float32
    )
    grad_returned = jnp.einsum(
        "ise,isd->eid", combine_low, grad_img, preferred_element_type=jnp.float32
    ).astype(jnp.bfloat16)
    grad_arrived = lax.all_to_all(grad_returned, "dp", split_axis=0, concat_axis=1, tiled=True)
    grad_rows = lax.all_gather(grad_arrived, "tensor", axis=1, tiled=True).reshape(-1, width)
    grad_second = jnp.einsum("rf,rd->fd", hidden, grad_rows, preferred_element_type=jnp.float32)
    grad_hidden = jnp.einsum(
        "rd,fd->rf", grad_rows, second_weight, preferred_element_type=jnp.float32
    )
    unused_value, gelu_back = jax.vjp(
        lambda values: jax.nn.gelu(values, approximate=False), pre_act
    )
    grad_pre = gelu_back(grad_hidden)[0].astype(jnp.bfloat16)
    grad_first = jnp.einsum("rd,rf->df", slot_rows, grad_pre, preferred_element_type=jnp.float32)
    slot_terms = jnp.einsum("rf,df->rd", grad_pre, first_weight, preferred_element_type=jnp.float32)
    grad_slot_rows = lax.psum_scatter(
        slot_terms.astype(jnp.bfloat16), "tensor", scatter_dimension=0, tiled=True
    )
    expert_in_grad = grad_first[None]
    expert_out_grad = grad_second[None]
    grad_slots = lax.all_to_all(
        grad_slot_rows.reshape(-1, images, width), "dp", split_axis=0, concat_axis=1, tiled=True
    ).reshape(experts, images, width)
    grad_dispatch = jnp.einsum(
        "isd,eid->ise", normed_img, grad_slots, preferred_element_type=jnp.float32
    )
    grad_normed = jnp.einsum(
        "ise,eid->isd", dispatch_low, grad_slots, preferred_element_type=jnp.float32
    )
    grad_logit_d = dispatch * (
        grad_dispatch - jnp.sum(grad_dispatch * dispatch, axis=1, keepdims=True)
    )
    grad_logit_c = combine * (grad_combine - jnp.sum(grad_combine * combine, axis=2, keepdims=True))
    grad_logits = (grad_logit_d + grad_logit_c).astype(jnp.bfloat16).reshape(own_rows, experts)
    grad_router = jnp.einsum(
        "rd,re->de", normed_two, grad_logits, preferred_element_type=jnp.float32
    )
    grad_two = grad_normed.reshape(own_rows, width) + jnp.einsum(
        "re,de->rd", grad_logits, router_full, preferred_element_type=jnp.float32
    )
    gain_two = jnp.sum(grad_two * unit_two, axis=0)
    shift_two = jnp.sum(grad_two, axis=0)
    grad_resid = grad_output + norm_back(grad_two, unit_two, inv_two, norms[2])
    grad_attn = grad_resid.astype(jnp.bfloat16)
    grad_attn_rows = lax.all_gather(grad_attn, "tensor", axis=0, tiled=True)
    grad_out_w = jnp.einsum(
        "rc,rd->cd", mixed_heads, grad_attn_rows, preferred_element_type=jnp.float32
    )
    grad_mixed = jnp.einsum(
        "rd,cd->rc", grad_attn_rows, out_use, preferred_element_type=jnp.float32
    ).astype(jnp.bfloat16)
    grad_proj = attention_backward(shaped, grad_mixed, log_totals, scale)
    grad_qkv = jnp.einsum("rd,krc->kdc", normed_one, grad_proj, preferred_element_type=jnp.float32)
    grad_one = jnp.einsum("krc,kdc->rd", grad_proj, qkv_use, preferred_element_type=jnp.float32)
    gain_one = jnp.sum(grad_one * unit_one, axis=0)
    shift_one = jnp.sum(grad_one, axis=0)
    grad_in_part = norm_back(grad_one, unit_one, inv_one, norms[0])
    small_grads = jnp.stack([gain_one, shift_one, gain_two, shift_two])
    grad_in_own, router_share, small_share = (
        lax.psum_scatter(
            grad_in_part.astype(jnp.bfloat16), "tensor", scatter_dimension=0, tiled=True
        ).astype(jnp.float32),
        lax.psum_scatter(
            grad_router.astype(jnp.bfloat16), "tensor", scatter_dimension=0, tiled=True
        ).astype(jnp.float32),
        lax.psum_scatter(
            small_grads.astype(jnp.bfloat16), "tensor", scatter_dimension=0, tiled=True
        ).astype(jnp.float32),
    )
    qkv_share, out_share = (grad_qkv, grad_out_w)
    input_grad = grad_resid + grad_in_own
    qkv_grad, out_grad, router_grad, norm_grad = (
        lax.psum_scatter(qkv_share, "dp", scatter_dimension=1, tiled=True),
        lax.psum_scatter(out_share, "dp", scatter_dimension=1, tiled=True),
        lax.psum_scatter(router_share, "dp", scatter_dimension=1, tiled=True),
        lax.psum_scatter(small_share, "dp", scatter_dimension=1, tiled=True),
    )
    return (
        output,
        input_grad,
        qkv_grad,
        out_grad,
        router_grad,
        norm_grad,
        expert_in_grad,
        expert_out_grad,
    )


def solution(mesh):
    placed = (
        P(("dp", "tensor"), None),
        P(None, "dp", "tensor"),
        P("tensor", "dp"),
        P("tensor", "dp"),
        P("tensor", "dp"),
        P("dp", None, "tensor"),
        P("dp", "tensor", None),
        P(("dp", "tensor"), None),
    )
    return jax.shard_map(
        on_device,
        mesh=mesh,
        in_specs=placed,
        out_specs=(
            P(("dp", "tensor"), None),
            P(("dp", "tensor"), None),
            P(None, "dp", "tensor"),
            P("tensor", "dp"),
            P("tensor", "dp"),
            P("tensor", "dp"),
            P("dp", None, "tensor"),
            P("dp", "tensor", None),
        ),
        check_vma=False,
    )
```

profile of v0, /device:TPU:0, one launch (start us, length us, event | category | flops | bytes accessed | tf_op | source)
XLA Modules:
  0.0 908.7 jit_solution(1507032761729864549)
XLA Ops:
  10.9 23.1 %all-reduce = bf16[768]{0:T(1024)(128)(2,1)S(1)} all-reduce(bf16[768]{0:T(1024)(128)(2,1)S(1)} %dynamic-update-slice), channel_id=1, replica_groups=mesh['dp'=8,'tensor'=4] {'dp'}, use_global_device_ids=true, to_apply=%add | all-reduce | flops 768 | bytes 3072
  41.1 36.3 %all_gather.33 = bf16[3,768,192]{2,0,1:T(4,128)(2,1)S(1)} all-gather(bf16[3,96,192]{2,0,1:T(4,128)(2,1)S(1)} %copy.67), channel_id=1, replica_groups=mesh['dp'=8,'tensor'=4] {'dp'}, dimensions={1}, use_global_device_ids=true | all-gather | bytes 995328 | tf_op jit(solution)/shard_map/all_gather | solution.py:122
  79.5 33.1 %all_gather.34 = bf16[192,768]{0,1:T(8,128)(2,1)} all-gather(bf16[192,96]{0,1:T(8,128)(2,1)S(1)} %copy.73), channel_id=1, replica_groups=mesh['dp'=8,'tensor'=4] {'dp'}, dimensions={1}, use_global_device_ids=true | all-gather | bytes 331776 | tf_op jit(solution)/shard_map/all_gather | solution.py:123
  116.9 9.9 %reshape.183 = f32[4728,768]{1,0:T(8,128)} reshape(bf16[4,1182,768]{2,1,0:T(8,128)(2,1)} %all-gather.8.cloned.1.call-done) | data formatting | bytes 21786624 | tf_op jit(solution)/shard_map/convert_element_type | solution.py:134
  126.8 6.8 multiply_reduce_fusion.3
  133.6 7.2 add_convert_fusion
  140.8 7.3 fusion.105
  154.9 8.1 squeeze.44
  166.7 9.2 %squeeze.43 = bf16[8,3,197,3,64]{2,1,0,4,3:T(4,128)(2,1)} reshape(bf16[1,4728,192]{1,2,0:T(8,128)(2,1)} %get-tuple-element.215) | data formatting | bytes 3631104 | tf_op jit(solution)/shard_map/squeeze | solution.py:96
  181.0 9.2 %squeeze.42 = bf16[8,3,197,3,64]{2,1,0,4,3:T(4,128)(2,1)} reshape(bf16[1,4728,192]{1,2,0:T(8,128)(2,1)} %get-tuple-element.216) | data formatting | bytes 3631104 | tf_op jit(solution)/shard_map/squeeze | solution.py:96
  197.0 37.2 %while.26 = (s32[]{:T(128)}, bf16[8,3,197,3,64]{2,4,3,1,0:T(8,128)(2,1)}, f32[8,3,3,197,1]{3,2,1,4,0:T(4,128)}, bf16[8,3,197,3,64]{2,4,3,1,0:T(8,128)(2,1)}, bf1...) while((s32[]{:T(128)}, bf16[8,3,197,3,64]{2,4,3,1,0:T(8,128)(2,1)}, ...), condition=%wide.region_5.6_spmd, body=%wide.region_2.5_spmd.sunk | while | flops 92671168 | bytes 5435089 | solution.py:94
  246.9 6.6 convolution_convert_fusion.2
  253.5 65.4 %fusion = bf16[1184,768]{1,0:T(8,128)(2,1)S(1)} fusion(bf16[4728,768]{1,0:T(8,128)(2,1)} %convolution_convert_fusion.2), kind=kCustom, calls=%all-reduce-scatter | all-reduce-scatter fusion | flops 3637249 | bytes 9081344
  320.2 18.5 %all-gather.2 = bf16[8,1,192]{2,1,0:T(2,128)(2,1)S(1)} all-gather(bf16[1,1,192]{2,1,0:T(2,128)(2,1)S(1)} %bitcast.246), channel_id=1, replica_groups=mesh['dp'=8,'tensor'=4] {'dp'}, dimensions={0}, use_global_device_ids=true | all-gather | bytes 3456 | tf_op jit(solution)/shard_map/all_gather | solution.py:124
  348.3 10.4 %concatenate.1 = bf16[1190,768]{1,0:T(8,128)(2,1)} concatenate(bf16[6,768]{1,0:T(8,128)(2,1)S(1)} %collective-permute-done, bf16[1184,768]{1,0:T(8,128)(2,1)} %copy-done.11), dimensions={0} | concatenate | bytes 3655680
  407.0 10.6 %reduce-scatter.19.cloned.1.call-done = bf16[48,768]{1,0:T(8,128)(2,1)} async-done(((bf16[192,768]{1,0:T(8,128)(2,1)}), bf16[48,768]{1,0:T(8,128)(2,1)}) %reduce-scatter.19.cloned.1.call-update) | async-done | bytes 73744 | tf_op jit(solution)/shard_map/reduce_scatter | solution.py:165
  424.7 16.5 %reduce-scatter.21.cloned.1.call-done = bf16[48,768]{1,0:T(8,128)(2,1)} async-done(((bf16[192,768]{1,0:T(8,128)(2,1)}), bf16[48,768]{1,0:T(8,128)(2,1)}) %reduce-scatter.21.cloned.1.call-update) | async-done | bytes 73744 | tf_op jit(solution)/shard_map/reduce_scatter | solution.py:193
  488.8 18.2 %all-reduce.3 = f32[192,8]{0,1:T(8,128)S(1)} all-reduce(bf16[192,8]{0,1:T(8,128)(2,1)S(1)} %copy.103), channel_id=9, replica_groups=mesh['dp'=8,'tensor'=4] {'dp'}, use_global_device_ids=true, to_apply=%region_28.29.clone | all-reduce | flops 1536 | bytes 9216
  507.0 25.7 %all-gather.10.cloned.1.call-done = bf16[4,1182,768]{2,1,0:T(8,128)(2,1)} async-done(((bf16[1,1182,768]{2,1,0:T(8,128)(2,1)}), bf16[4,1182,768]{2,1,0:T(8,128)(2,1)}) %all-gather.10.cloned.1.call-update) | async-done | bytes 7262224 | tf_op jit(solution)/shard_map/all_gather | solution.py:222
  532.7 7.9 reshape.182
  546.0 8.4 reshape.169
  563.1 76.3 %while.27 = (s32[]{:T(128)}, bf16[8,3,197,3,64]{2,4,3,1,0:T(8,128)(2,1)}, bf16[8,3,197,3,64]{2,4,3,1,0:T(8,128)(2,1)}, bf16[8,3,197,3,64]{2,4,3,1,0:T(8,128)(2,1...) while((s32[]{:T(128)}, ...), condition=%wide.region_21.22_spmd, body=%wide.region_19.21_spmd.sunk | while | flops 226899664 | bytes 13914319 | solution.py:105
  644.8 6.6 stack.34
  655.0 6.8 stack.32
  676.3 18.3 %fusion.48 = (bf16[768]{0:T(1024)(128)(2,1)S(1)}, f32[4728]{0:T(1024)S(1)}, f32[4728]{0:T(1024)S(1)}, bf16[768]{0:T(1024)(128)(2,1)S(1)}, f32[4728,768,1]{1,0,2:T(8,128)}) fusion(f32[4728,768]{1,0:T(8,128)} %reshape.183, f32[4728]{0:T(1024)S(1)} %copy-done.31, f32[4728]{0:T(1024)S(1)} %copy-done.29, f32[768]{0:T(1024)S(1)} %copy-done.41, ...), kind=kOutput, calls=%fused_computation.61 | convolution fusion | flops 4215700992 | bytes 35462016 | tf_op jit(solution)/shard_map/krc,kdc->rd/dot_general | solution.py:231
  702.4 6.9 convolution_bitcast_fusion.2
  709.4 8.7 fusion.53
  725.5 13.2 %multiply_convert_fusion.1 = bf16[4728,768]{1,0:T(8,128)(2,1)} fusion(f32[4728,768,1]{1,0,2:T(8,128)} %get-tuple-element.226, f32[4728,768]{1,0:T(8,128)} %reshape.183, f32[4728]{0:T(1024)S(1)} %broadcast_multiply_fusion.2, f32[4728]{0:T(1024)S(1)} %broadcast_multiply_fusion.1, f32[768]{0:T(1024)S(1)} %copy-done.41, f32[4728]{0:T(1024)S(1)} %copy-done.31, ...), kind=kLoop, calls=%fused_computation.62 | loop fusion | flops 29048832 | bytes 36389760 | tf_op jit(solution)/shard_map/convert_element_type | solution.py:238
  738.8 65.3 %fusion.1 = bf16[1184,768]{1,0:T(8,128)(2,1)S(1)} fusion(bf16[4728,768]{1,0:T(8,128)(2,1)} %multiply_convert_fusion.1), kind=kCustom, calls=%all-reduce-scatter.1 | all-reduce-scatter fusion | flops 3637249 | bytes 9081344
  807.9 8.5 concatenate.2
  821.5 8.3 reduce-scatter.25.cloned.1.call-done
  831.4 68.0 %reduce-scatter.23.cloned.1.call-done = f32[96,576]{1,0:T(8,128)} async-done(((f32[768,576]{1,0:T(8,128)}), f32[96,576]{1,0:T(8,128)}) %reduce-scatter.23.cloned.1.call-update) | async-done | bytes 221200
  (316 shorter events, 342.6 us)
Async XLA Ops:
  7.2 385.1 %copy-start = (bf16[1,768,768]{2,1,0:T(8,128)(2,1)S(1)}, bf16[1,768,768]{2,1,0:T(8,128)(2,1)}, u32[]{:S(2)}) copy-start(bf16[1,768,768]{2,1,0:T(8,128)(2,1)} %param.17) | copy-start | bytes 3538948
  7.2 105.5 %all-gather.8.cloned.1.call-start = ((), (), s32[]{:S(2)}) async-start(), calls=%async_computation.12 | async-start | bytes 9093120 | tf_op jit(solution)/shard_map/all_gather | solution.py:128
  79.5 54.1 %copy-start.40 = (f32[768]{0:T(1024)}, f32[768]{0:T(1024)S(1)}, u32[]{:S(2)}) copy-start(f32[768]{0:T(1024)S(1)} %get-tuple-element.172) | copy-start | bytes 9220
  79.5 282.9 %copy-start.42 = (f32[768]{0:T(1024)}, f32[768]{0:T(1024)S(1)}, u32[]{:S(2)}) copy-start(f32[768]{0:T(1024)S(1)} %get-tuple-element.173) | copy-start | bytes 9220
  116.9 16.7 %copy-start.28 = (f32[4728]{0:T(1024)}, f32[4728]{0:T(1024)S(1)}, u32[]{:S(2)}) copy-start(f32[4728]{0:T(1024)S(1)} %reshape.200) | copy-start | bytes 56740
  133.6 7.2 copy-start.30
  140.8 7.3 copy-start.16
  253.5 66.7 %copy-start.44 = (bf16[192,1]{0,1:T(2,128)(2,1)S(1)}, bf16[192,1]{0,1:T(2,128)(2,1)}, u32[]{:S(2)}) copy-start(bf16[192,1]{0,1:T(2,128)(2,1)} %param.15) | copy-start | bytes 1156
  318.9 25.4 %copy-start.11 = (bf16[1184,768]{1,0:T(8,128)(2,1)}, bf16[1184,768]{1,0:T(8,128)(2,1)S(1)}, u32[]{:S(2)}) copy-start(bf16[1184,768]{1,0:T(8,128)(2,1)S(1)} %fusion) | copy-start | bytes 5455876
  318.9 29.4 %collective-permute-start = (bf16[6,768]{1,0:T(8,128)(2,1)S(1)}, bf16[6,768]{1,0:T(8,128)(2,1)S(1)}, u32[]{:S(2)}, u32[]{:S(2)}) collective-permute-start(bf16[6,768]{1,0:T(8,128)(2,1)S(1)} %slice.47), channel_id=1, source_target_pairs={{0,1},{1,2},{2,3},{4,5},{5,6},{6,7},{8,9},{9,10},{10,11},{12,13},{... | collective-permute-start | bytes 27656
  344.3 19.3 %copy-start.36 = (bf16[768,8]{0,1:T(8,128)(2,1)}, bf16[768,8]{0,1:T(8,128)(2,1)S(1)}, u32[]{:S(2)}) copy-start(bf16[768,8]{0,1:T(8,128)(2,1)S(1)} %reshape.180) | copy-start | bytes 36868
  347.5 11.2 %copy-start.2 = (bf16[1182,768]{1,0:T(8,128)(2,1)S(1)}, bf16[1182,768]{1,0:T(8,128)(2,1)}, u32[]{:S(2)}) copy-start(bf16[1182,768]{1,0:T(8,128)(2,1)} %param.12) | copy-start | bytes 5446660
  368.9 13.5 %copy-start.32 = (f32[6,197]{1,0:T(8,128)}, f32[6,197]{1,0:T(8,128)S(1)}, u32[]{:S(2)}) copy-start(f32[6,197]{1,0:T(8,128)S(1)} %div.54) | copy-start | bytes 14188
  371.9 10.6 %all-to-all-start = ((bf16[8,6,768]{2,1,0:T(8,128)(2,1)}), bf16[8,6,768]{2,1,0:T(8,128)(2,1)S(1)}, u32[]{:S(2)}, u32[]{:S(2)}) async-start(bf16[8,6,768]{2,1,0:T(8,128)(2,1)} %copy.78), calls=%async_computation | async-start | bytes 196608 | tf_op jit(solution)/shard_map/all_to_all | solution.py:158
  382.4 13.5 %all-to-all-start.2 = ((bf16[8,6,768]{2,1,0:T(8,128)(2,1)}), bf16[8,6,768]{2,1,0:T(8,128)(2,1)S(1)}, u32[]{:S(2)}, u32[]{:S(2)}) async-start(bf16[8,6,768]{2,1,0:T(8,128)(2,1)} %copy.80), calls=%async_computation.3 | async-start | bytes 196608 | tf_op jit(solution)/shard_map/all_to_all | solution.py:181
  385.8 31.8 %reduce-scatter.19.cloned.1.call-start = ((), (), s32[]{:S(2)}) async-start(), calls=%async_computation.10 | async-start | bytes 368640 | tf_op jit(solution)/shard_map/reduce_scatter | solution.py:165
  395.9 45.3 %reduce-scatter.21.cloned.1.call-start = ((), (), s32[]{:S(2)}) async-start(), calls=%async_computation.11 | async-start | bytes 368640 | tf_op jit(solution)/shard_map/reduce_scatter | solution.py:193
  405.7 44.6 %copy-start.33 = (f32[6,197]{1,0:T(8,128)S(1)}, f32[6,197]{1,0:T(8,128)}, u32[]{:S(2)}) copy-start(f32[6,197]{1,0:T(8,128)} %copy-done.32) | copy-start | bytes 14188
  419.2 23.6 %all-to-all-start.1 = ((bf16[8,6,768]{2,1,0:T(8,128)(2,1)}), bf16[8,6,768]{2,1,0:T(8,128)(2,1)S(1)}, u32[]{:S(2)}, u32[]{:S(2)}) async-start(bf16[8,6,768]{2,1,0:T(8,128)(2,1)} %reshape.162), calls=%async_computation.2 | async-start | bytes 196608 | tf_op jit(solution)/shard_map/all_to_all | solution.py:168
  424.7 32.7 %copy-start.35 = (f32[6,8]{1,0:T(8,128)S(1)}, f32[6,8]{1,0:T(8,128)}, u32[]{:S(2)}) copy-start(f32[6,8]{1,0:T(8,128)} %copy-done.34) | copy-start | bytes 580
  424.7 32.7 %copy-start.39 = (f32[6,8]{1,0:T(8,128)S(1)}, f32[6,8]{1,0:T(8,128)}, u32[]{:S(2)}) copy-start(f32[6,8]{1,0:T(8,128)} %copy-done.38) | copy-start | bytes 580
  442.7 12.6 %all-to-all-start.3 = ((bf16[8,6,768]{2,1,0:T(8,128)(2,1)}), bf16[8,6,768]{2,1,0:T(8,128)(2,1)S(1)}, u32[]{:S(2)}, u32[]{:S(2)}) async-start(bf16[8,6,768]{2,1,0:T(8,128)(2,1)} %reshape.166), calls=%async_computation.5 | async-start | bytes 196608 | tf_op jit(solution)/shard_map/all_to_all | solution.py:198
  448.2 39.7 %reduce-scatter.27.cloned.1.call-start = ((), (), s32[]{:S(2)}) async-start(), calls=%async_computation.16 | async-start | bytes 245760
  460.4 72.3 %all-gather.10.cloned.1.call-start = ((), (), s32[]{:S(2)}) async-start(), calls=%async_computation.13 | async-start | bytes 9093120 | tf_op jit(solution)/shard_map/all_gather | solution.py:222
  483.9 322.6 %reduce-scatter.29.cloned.1.call-start = ((), (), s32[]{:S(2)}) async-start(), calls=%async_computation.17 | async-start | bytes 442368
  507.0 33.6 %copy-start.17 = (bf16[192,768]{0,1:T(8,128)(2,1)S(1)}, bf16[192,768]{0,1:T(8,128)(2,1)}, u32[]{:S(2)}) copy-start(bf16[192,768]{0,1:T(8,128)(2,1)} %all_gather.34) | copy-start | bytes 884740
  676.3 18.4 %copy-start.27 = (bf16[3,4728,192]{1,2,0:T(8,128)(2,1)}, bf16[3,4728,192]{1,2,0:T(8,128)(2,1)S(1)}, u32[]{:S(2)}) copy-start(bf16[3,4728,192]{1,2,0:T(8,128)(2,1)S(1)} %constant_dynamic-update-slice_fusion) | copy-start | bytes 16339972
  676.3 26.2 %copy-start.8 = (bf16[4728,192]{0,1:T(8,128)(2,1)S(1)}, bf16[4728,192]{0,1:T(8,128)(2,1)}, u32[]{:S(2)}) copy-start(bf16[4728,192]{0,1:T(8,128)(2,1)} %reshape.158) | copy-start | bytes 5446660
  702.4 127.4 %reduce-scatter.25.cloned.1.call-start = ((), (), s32[]{:S(2)}) async-start(), calls=%async_computation.15 | async-start | bytes 884736
  709.4 190.1 %reduce-scatter.23.cloned.1.call-start = ((), (), s32[]{:S(2)}) async-start(), calls=%async_computation.14 | async-start | bytes 2211840
  804.0 3.9 collective-permute-start.1
  816.4 84.9 %copy-start.1 = (bf16[1,768,768]{2,1,0:T(8,128)(2,1)S(1)}, bf16[1,768,768]{2,1,0:T(8,128)(2,1)}, u32[]{:S(2)}) copy-start(bf16[1,768,768]{2,1,0:T(8,128)(2,1)} %param.17) | copy-start | bytes 3538948
  (27 other events, 89.0 us)
Sparse Core Ops, SparseCore 0:
  9.6 54.7 all-gather.7
  396.0 21.5 reduce-scatter.18
  420.8 20.2 reduce-scatter.20
  460.5 16.4 reduce-scatter.26
  484.1 48.6 all-gather.9
  702.5 62.4 reduce-scatter.28
  768.3 61.4 reduce-scatter.24
  833.7 65.7 reduce-scatter.22
where the time goes:
time: 919 us; the launch traced here: 909 us
  blocking collectives  289 us (31%)
  local copies, waits for them, and re-layouts  199 us (22%)
  matrix products  181 us (20%)
  waiting for transfers between devices  139 us (15%)
  other arithmetic  63.1 us (7%)
  starting transfers between devices  20.8 us (2%)
  between operations  16.8 us (2%)
    unnamed x5, blocking collectives  178 us
    unnamed x14, waiting for transfers between devices  77.1 us
    unnamed x115, local copies, waits for them, and re-layouts  53.9 us
    all_gather x1, blocking collectives, on_device(): lax.all_gather(qkv_weight, 'dp', axis=1, tiled=True)  36.3 us
    all_gather x1, blocking collectives, on_device(): lax.all_gather(out_weight, 'dp', axis=1, tiled=True)  33.1 us
    all_gather x1, waiting for transfers between devices, on_device(): grad_attn_rows = lax.all_gather(grad_attn, 'tensor', axis=0, tiled=True)  25.7 us
    another operation x4, local copies, waits for them, and re-layouts, attention_backward(): stacked = jnp.stack(grad_parts)  20.2 us
    while x4, local copies, waits for them, and re-layouts, attention_forward(): lax.map(lambda pieces: attend_forward(pieces[0], pieces[1], pieces[2], sc...  20 us
  transfers between devices with their start and end apart: 14, of which 7 were waited for; matrix products, arithmetic and copies ran while one was open for 19% of the time, Pallas kernels for 0%

commit v1 on v0

v1 whole, which is shorter than its diff:
```python
import functools

import jax
import jax.numpy as jnp
from jax import lax
from jax.experimental import pallas as pl
from jax.experimental.pallas import tpu as pltpu
from jax.sharding import PartitionSpec as P

HEAD_DIM = 64
SEQ = 197
PAD = 208
SLOT_ROWS = 16
AXES = ("dp", "tensor")
BF = jnp.bfloat16
F32 = jnp.float32
LAST = (((1,), (1,)), ((), ()))
FIRST = (((0,), (0,)), ((), ()))
MIDDLE = (((1,), (0,)), ((), ()))
VMEM_LIMIT = 56 * 1024 * 1024


def dot(a, b, dims=MIDDLE):
    return lax.dot_general(a, b, dims, preferred_element_type=F32)


def params():
    return pltpu.CompilerParams(vmem_limit_bytes=VMEM_LIMIT)


def whole(shape):
    return pl.BlockSpec(shape, lambda i: (0,) * len(shape))


def per_image(shape, column=0):
    return pl.BlockSpec((1,) + shape, lambda i: (i, 0, column))


def layer_stats(values):
    centre = jnp.mean(values, axis=-1, keepdims=True)
    centred = values - centre
    spread = jnp.mean(centred * centred, axis=-1, keepdims=True)
    inv_std = lax.rsqrt(spread + 1e-06)
    return centred * inv_std, inv_std


def lane_ids(shape):
    return lax.broadcasted_iota(jnp.int32, shape, len(shape) - 1)


def row_ids(shape):
    return lax.broadcasted_iota(jnp.int32, shape, len(shape) - 2)


def norm_kernel(x_ref, norms_ref, out_ref):
    unit, _ = layer_stats(x_ref[0].astype(F32))
    out_ref[0] = (unit * norms_ref[0:1, :] + norms_ref[1:2, :]).astype(BF)


def first_norm(x_img, norms):
    images, rows, width = x_img.shape
    return pl.pallas_call(
        norm_kernel,
        grid=(images,),
        in_specs=[per_image((rows, width)), whole(norms.shape)],
        out_specs=per_image((rows, width)),
        out_shape=jax.ShapeDtypeStruct((images, rows, width), BF),
        compiler_params=params(),
        name="first_norm",
    )(x_img, norms)


def attend_kernel(pairs, n_ref, w_ref, qkv_ref, mixed_ref, probs_ref):
    span = pairs * 128
    rows = n_ref.shape[1]
    proj = dot(n_ref[0], w_ref[...])
    low = lane_ids((rows, 128)) < HEAD_DIM
    key_ok = row_ids((rows, rows)) < SEQ
    zero = jnp.zeros((rows, 128), BF)
    for p in range(pairs):
        at = slice(p * 128, (p + 1) * 128)
        q = (proj[:, p * 128 : (p + 1) * 128] * HEAD_DIM ** (-0.5)).astype(BF)
        k = proj[:, span + p * 128 : span + (p + 1) * 128].astype(BF)
        v = proj[:, 2 * span + p * 128 : 2 * span + (p + 1) * 128].astype(BF)
        qkv_ref[0, :, at] = q
        qkv_ref[0, :, span + p * 128 : span + (p + 1) * 128] = k
        qkv_ref[0, :, 2 * span + p * 128 : 2 * span + (p + 1) * 128] = v
        v_t = v.T
        mixed_t = []
        for h in range(2):
            q_one = jnp.where(low, q, zero) if h == 0 else jnp.where(low, zero, q)
            scores = jnp.where(key_ok, dot(k, q_one, LAST), -1e30)
            highest = jnp.max(scores, axis=0, keepdims=True)
            scaled = jnp.exp(scores - highest)
            inv = 1.0 / jnp.sum(scaled, axis=0, keepdims=True)
            weights = (scaled * inv).astype(BF)
            probs_ref[0, 2 * p + h] = weights
            mixed_t.append(dot(v_t[h * HEAD_DIM : (h + 1) * HEAD_DIM, :], weights))
        mixed_ref[0, :, at] = jnp.concatenate(mixed_t, axis=0).T.astype(BF)


def attend(normed, weights):
    images, rows, width = normed.shape
    span = weights.shape[1] // 3
    heads = span // HEAD_DIM
    return pl.pallas_call(
        functools.partial(attend_kernel, span // 128),
        grid=(images,),
        in_specs=[per_image((rows, width)), whole(weights.shape)],
        out_specs=[
            per_image((rows, 3 * span)),
            per_image((rows, span)),
            pl.BlockSpec((1, heads, rows, rows), lambda i: (i, 0, 0, 0)),
        ],
        out_shape=[
            jax.ShapeDtypeStruct((images, rows, 3 * span), BF),
            jax.ShapeDtypeStruct((images, rows, span), BF),
            jax.ShapeDtypeStruct((images, heads, rows, rows), BF),
        ],
        compiler_params=params(),
        name="attend",
    )(normed, weights)


def softmaxes(logits):
    ok = lane_ids(logits.shape) < SEQ
    masked = jnp.where(ok, logits, -1e30)
    up = jnp.exp(masked - jnp.max(masked, axis=1, keepdims=True))
    dispatch = up / jnp.sum(up, axis=1, keepdims=True)
    up = jnp.exp(logits - jnp.max(logits, axis=0, keepdims=True))
    combine = up / jnp.sum(up, axis=0, keepdims=True)
    return dispatch, combine


def place_rows(experts, image, offset):
    shape = (experts * SLOT_ROWS, experts)
    return (row_ids(shape) == lane_ids(shape) * SLOT_ROWS + offset + image).astype(BF)


def pick_rows(experts, image, offset):
    shape = (experts, experts * SLOT_ROWS)
    return (lane_ids(shape) == row_ids(shape) * SLOT_ROWS + offset + image).astype(BF)


def route_kernel(
    half, x_ref, m1_ref, m2_ref, out_w_ref, norms_ref, router_ref, g_ref, y_ref, logits_ref, send_ref, acc
):
    image = pl.program_id(0)
    experts = router_ref.shape[0]
    out_w = out_w_ref[...]
    attn = dot(m1_ref[0], out_w[:, :half], LAST) + dot(m2_ref[0], out_w[:, half:], LAST)
    y = x_ref[0].astype(F32) + attn
    y_ref[0] = y
    unit, _ = layer_stats(y)
    normed = (unit * norms_ref[2:3, :] + norms_ref[3:4, :]).astype(BF)
    logits = dot(router_ref[...], normed, LAST)
    logits_ref[0] = logits
    dispatch, combine = softmaxes(logits)
    slots = dot(dispatch.astype(BF), normed).astype(BF)
    grad_returned = dot(combine.astype(BF), g_ref[0]).astype(BF)
    placed = dot(place_rows(experts, image, 0), slots) + dot(
        place_rows(experts, image, SLOT_ROWS // 2), grad_returned
    )

    @pl.when(image == 0)
    def _():
        acc[...] = placed

    @pl.when(image > 0)
    def _():
        acc[...] += placed

    @pl.when(image == pl.num_programs(0) - 1)
    def _():
        send_ref[...] = acc[...].astype(BF)


def route(x_img, mixed_one, mixed_two, out_w, norms, router, g_img):
    images, rows, width = x_img.shape
    experts = router.shape[0]
    half = mixed_one.shape[2]
    return pl.pallas_call(
        functools.partial(route_kernel, half),
        grid=(images,),
        in_specs=[
            per_image((rows, width)),
            per_image((rows, half)),
            per_image((rows, width - half)),
            whole(out_w.shape),
            whole(norms.shape),
            whole(router.shape),
            per_image((rows, width)),
        ],
        out_specs=[
            per_image((rows, width)),
            per_image((experts, rows)),
            whole((experts * SLOT_ROWS, width)),
        ],
        out_shape=[
            jax.ShapeDtypeStruct((images, rows, width), F32),
            jax.ShapeDtypeStruct((images, experts, rows), F32),
            jax.ShapeDtypeStruct((experts * SLOT_ROWS, width), BF),
        ],
        scratch_shapes=[pltpu.VMEM((experts * SLOT_ROWS, width), F32)],
        compiler_params=params(),
        name="route",
    )(x_img, mixed_one, mixed_two, out_w, norms, router, g_img)


def split_rows(blocks):
    wide = blocks.astype(F32)
    half = SLOT_ROWS // 2
    flat = (blocks.shape[0] * half, blocks.shape[2])
    return wide[:, :half].reshape(flat).astype(BF), wide[:, half:].reshape(flat).astype(BF)


def join_rows(ones, twos):
    half = SLOT_ROWS // 2
    shape = (ones.shape[0] // half, half, ones.shape[1])
    return jnp.concatenate([ones.reshape(shape), twos.reshape(shape)], axis=1).astype(BF)


def gelu_parts(pre):
    cdf = 0.5 * (1.0 + lax.erf(pre * (0.5**0.5)))
    density = jnp.exp(-0.5 * pre * pre) * 0.3989422804014327
    return pre * cdf, cdf + pre * density


def expert_kernel(own_ref, near_ref, w1_ref, w2_ref, keep_ref, send_ref, d1_ref, d2_ref):
    count = own_ref.shape[0]
    blocks = jnp.concatenate([own_ref[...], near_ref[...]], axis=0)
    slots, grads = split_rows(blocks)
    pre = dot(slots, w1_ref[...])
    hidden, slope = gelu_parts(pre)
    hidden = hidden.astype(BF)
    returned = dot(hidden, w2_ref[...])
    grad_pre = (dot(grads, w2_ref[...], LAST) * slope).astype(BF)
    grad_slots = dot(grad_pre, w1_ref[...], LAST)
    joined = join_rows(returned, grad_slots)
    keep_ref[...] = joined[:count]
    send_ref[...] = joined[count:]
    d1_ref[...] = dot(slots, grad_pre, FIRST)
    d2_ref[...] = dot(hidden, grads, FIRST)


def run_expert(own, near, first_weight, second_weight):
    width, units = first_weight.shape
    return pl.pallas_call(
        expert_kernel,
        out_shape=[
            jax.ShapeDtypeStruct(own.shape, BF),
            jax.ShapeDtypeStruct(near.shape, BF),
            jax.ShapeDtypeStruct((width, units), F32),
            jax.ShapeDtypeStruct((units, width), F32),
        ],
        compiler_params=params(),
        name="expert",
    )(own, near, first_weight, second_weight)


def moe_back_kernel(
    half,
    y_ref,
    g_ref,
    logits_ref,
    back_ref,
    norms_ref,
    router_ref,
    out_w_ref,
    m1_ref,
    m2_ref,
    out_ref,
    grad_y_ref,
    grad_mixed_ref,
    out_grad_ref,
    small_ref,
):
    image = pl.program_id(0)
    experts = router_ref.shape[0]
    y = y_ref[0]
    g_low = g_ref[0]
    back = back_ref[...]
    returned = dot(pick_rows(experts, image, 0), back).astype(BF)
    grad_slots = dot(pick_rows(experts, image, SLOT_ROWS // 2), back).astype(BF)
    dispatch, combine = softmaxes(logits_ref[0])
    unit, inv_std = layer_stats(y)
    gain = norms_ref[2:3, :]
    normed = (unit * gain + norms_ref[3:4, :]).astype(BF)
    out_ref[0] = (y + dot(combine.astype(BF), returned, FIRST)).astype(BF)
    grad_combine = dot(returned, g_low, LAST)
    grad_dispatch = dot(grad_slots, normed, LAST)
    grad_logits = dispatch * (
        grad_dispatch - jnp.sum(grad_dispatch * dispatch, axis=1, keepdims=True)
    ) + combine * (grad_combine - jnp.sum(grad_combine * combine, axis=0, keepdims=True))
    grad_logits = grad_logits.astype(BF)
    router_grad = dot(grad_logits, normed)
    grad_two = dot(dispatch.astype(BF), grad_slots, FIRST) + dot(grad_logits, router_ref[...], FIRST)
    gain_grad = jnp.sum(grad_two * unit, axis=0, keepdims=True)
    shift_grad = jnp.sum(grad_two, axis=0, keepdims=True)
    scaled = grad_two * gain
    mean_one = jnp.mean(scaled, axis=-1, keepdims=True)
    mean_two = jnp.mean(scaled * unit, axis=-1, keepdims=True)
    grad_y = g_low.astype(F32) + inv_std * (scaled - mean_one - unit * mean_two)
    grad_y_ref[0] = grad_y
    grad_attn = grad_y.astype(BF)
    grad_mixed_ref[0] = dot(grad_attn, out_w_ref[...]).astype(BF)

    @pl.when(image == 0)
    def _():
        out_grad_ref[...] = jnp.zeros_like(out_grad_ref)
        small_ref[...] = jnp.zeros_like(small_ref)

    out_grad_ref[:, :half] += dot(grad_attn, m1_ref[0], FIRST)
    out_grad_ref[:, half:] += dot(grad_attn, m2_ref[0], FIRST)
    small_ref[0:1, :] += gain_grad
    small_ref[1:2, :] += shift_grad
    small_ref[8 : 8 + experts, :] += router_grad


def moe_back(y, g_img, logits, back, norms, router, out_w, mixed_one, mixed_two):
    images, rows, width = y.shape
    experts = router.shape[0]
    half = mixed_one.shape[2]
    return pl.pallas_call(
        functools.partial(moe_back_kernel, half),
        grid=(images,),
        in_specs=[
            per_image((rows, width)),
            per_image((rows, width)),
            per_image((experts, rows)),
            whole(back.shape),
            whole(norms.shape),
            whole(router.shape),
            whole(out_w.shape),
            per_image((rows, half)),
            per_image((rows, width - half)),
        ],
        out_specs=[
            per_image((rows, width)),
            per_image((rows, width)),
            per_image((rows, width)),
            whole((width, width)),
            whole((8 + experts, width)),
        ],
        out_shape=[
            jax.ShapeDtypeStruct((images, rows, width), BF),
            jax.ShapeDtypeStruct((images, rows, width), F32),
            jax.ShapeDtypeStruct((images, rows, width), BF),
            jax.ShapeDtypeStruct((width, width), F32),
            jax.ShapeDtypeStruct((8 + experts, width), F32),
        ],
        compiler_params=params(),
        name="moe_back",
    )(y, g_img, logits, back, norms, router, out_w, mixed_one, mixed_two)


def attend_back_kernel(pairs, n_ref, qkv_ref, probs_ref, mixed_ref, gm_ref, grads_ref, dw_ref):
    image = pl.program_id(0)
    span = pairs * 128
    rows = n_ref.shape[1]
    low = lane_ids((rows, 128)) < HEAD_DIM
    zero = jnp.zeros((rows, 128), BF)
    minus = jnp.full((rows, 128), -1.0, BF)
    for p in range(pairs):
        at = slice(p * 128, (p + 1) * 128)
        q = qkv_ref[0, :, at]
        k = qkv_ref[0, :, span + p * 128 : span + (p + 1) * 128]
        v = qkv_ref[0, :, 2 * span + p * 128 : 2 * span + (p + 1) * 128]
        gm = gm_ref[0, :, at]
        inner = pltpu.roll(gm.astype(F32) * mixed_ref[0, :, at].astype(F32), HEAD_DIM, 1).astype(BF)
        k_t = k.T
        grad_q_t, grad_k, grad_v = [], 0.0, 0.0
        for h in range(2):
            mine = low if h == 0 else jnp.logical_not(low)
            weights = probs_ref[0, 2 * p + h]
            centred = dot(jnp.where(mine, v, minus), jnp.where(mine, gm, inner), LAST)
            grad_scores = (weights.astype(F32) * centred).astype(BF)
            grad_v = grad_v + dot(weights, jnp.where(mine, gm, zero))
            grad_k = grad_k + dot(grad_scores, jnp.where(mine, q, zero))
            grad_q_t.append(dot(k_t[h * HEAD_DIM : (h + 1) * HEAD_DIM, :], grad_scores))
        grad_q = jnp.concatenate(grad_q_t, axis=0).T * HEAD_DIM ** (-0.5)
        grads_ref[0, :, at] = grad_q.astype(BF)
        grads_ref[0, :, span + p * 128 : span + (p + 1) * 128] = grad_k.astype(BF)
        grads_ref[0, :, 2 * span + p * 128 : 2 * span + (p + 1) * 128] = grad_v.astype(BF)

    @pl.when(image == 0)
    def _():
        dw_ref[...] = jnp.zeros_like(dw_ref)

    dw_ref[...] += dot(n_ref[0], grads_ref[0], FIRST)


def attend_back(normed, qkv, probs, mixed, grad_mixed, piece):
    images, rows, width = normed.shape
    span = mixed.shape[2]
    heads = span // HEAD_DIM
    return pl.pallas_call(
        functools.partial(attend_back_kernel, span // 128),
        grid=(images,),
        in_specs=[
            per_image((rows, width)),
            per_image((rows, 3 * span)),
            pl.BlockSpec((1, heads, rows, rows), lambda i: (i, 0, 0, 0)),
            per_image((rows, span)),
            per_image((rows, span), piece),
        ],
        out_specs=[per_image((rows, 3 * span)), whole((width, 3 * span))],
        out_shape=[
            jax.ShapeDtypeStruct((images, rows, 3 * span), BF),
            jax.ShapeDtypeStruct((width, 3 * span), F32),
        ],
        compiler_params=params(),
        name="attend_back",
    )(normed, qkv, probs, mixed, grad_mixed)


def input_back_kernel(x_ref, gy_ref, p1_ref, p2_ref, w1_ref, w2_ref, norms_ref, out_ref, small_ref):
    image = pl.program_id(0)
    unit, inv_std = layer_stats(x_ref[0].astype(F32))
    grad_one = dot(p1_ref[0], w1_ref[...], LAST) + dot(p2_ref[0], w2_ref[...], LAST)
    scaled = grad_one * norms_ref[0:1, :]
    mean_one = jnp.mean(scaled, axis=-1, keepdims=True)
    mean_two = jnp.mean(scaled * unit, axis=-1, keepdims=True)
    out_ref[0] = gy_ref[0] + inv_std * (scaled - mean_one - unit * mean_two)

    @pl.when(image == 0)
    def _():
        small_ref[...] = jnp.zeros_like(small_ref)

    small_ref[0:1, :] += jnp.sum(grad_one * unit, axis=0, keepdims=True)
    small_ref[1:2, :] += jnp.sum(grad_one, axis=0, keepdims=True)


def input_back(x_img, grad_y, grads_one, grads_two, weight_one, weight_two, norms):
    images, rows, width = x_img.shape
    return pl.pallas_call(
        input_back_kernel,
        grid=(images,),
        in_specs=[
            per_image((rows, width)),
            per_image((rows, width)),
            per_image(grads_one.shape[1:]),
            per_image(grads_two.shape[1:]),
            whole(weight_one.shape),
            whole(weight_two.shape),
            whole(norms.shape),
        ],
        out_specs=[per_image((rows, width)), whole((8, width))],
        out_shape=[
            jax.ShapeDtypeStruct((images, rows, width), F32),
            jax.ShapeDtypeStruct((8, width), F32),
        ],
        compiler_params=params(),
        name="input_back",
    )(x_img, grad_y, grads_one, grads_two, weight_one, weight_two, norms)


def swap(value, dp_size, tensor_size, dp_mask, tensor_mask):
    pairs = [
        (d * tensor_size + t, (d ^ dp_mask) * tensor_size + (t ^ tensor_mask))
        for d in range(dp_size)
        for t in range(tensor_size)
    ]
    return lax.ppermute(value, AXES, pairs)


def steps_of(dp_size):
    bits = dp_size.bit_length() - 1
    down = list(range(bits))[::-1]
    return [down, down[-1:] + down[:-1]]


def step_pairs(dp_size, tensor_size, step):
    orders = steps_of(dp_size)
    return [
        (d * tensor_size + t, (d ^ (1 << orders[t % 2][step])) * tensor_size + t)
        for d in range(dp_size)
        for t in range(tensor_size)
    ]


def places(dp_size, dp_index, core):
    away = dp_index ^ jnp.arange(dp_size, dtype=jnp.int32)
    both = []
    for order in steps_of(dp_size):
        at = jnp.zeros_like(away)
        for step, bit in enumerate(order):
            at = at | (((away >> bit) & 1) << step)
        both.append(at)
    return jnp.where(core == 0, both[0], both[1]), jnp.where(core == 0, both[1], both[0])


def gather_steps(block, dp_size, tensor_size):
    held = block[None]
    for step in range(dp_size.bit_length() - 1):
        got = lax.ppermute(held, AXES, step_pairs(dp_size, tensor_size, step))
        held = jnp.concatenate([held, got], axis=0)
    return held


def scatter_steps(blocks, dp_size, tensor_size):
    held = blocks
    for step in range(dp_size.bit_length() - 1)[::-1]:
        half = 1 << step
        got = lax.ppermute(held[half:], AXES, step_pairs(dp_size, tensor_size, step))
        held = (held[:half].astype(F32) + got.astype(F32)).astype(BF)
    return held[0]


def assemble_kernel(part, core_ref, own_place, sib_place, own_ref, sib_ref, out_ref):
    core = core_ref[0]
    for k in range(own_ref.shape[0]):
        for place, ref, which in ((own_place, own_ref, core), (sib_place, sib_ref, 1 - core)):
            row = pl.multiple_of(2 * part * k + part * which, 16)
            out_ref[pl.ds(row, part), :] = ref[place[k], 0:part, :]


def assemble(own, sib, part, core, own_place, sib_place):
    return pl.pallas_call(
        functools.partial(assemble_kernel, part),
        in_specs=[pl.BlockSpec(memory_space=pltpu.SMEM)] * 3 + [pl.BlockSpec(memory_space=pltpu.VMEM)] * 2,
        out_shape=jax.ShapeDtypeStruct((own.shape[0] * 2 * part, own.shape[2]), BF),
        compiler_params=params(),
        name="assemble",
    )(core, own_place, sib_place, own, sib)


def deal_kernel(part, core_ref, own_place, sib_place, full_ref, own_ref, sib_ref):
    core = core_ref[0]
    for k in range(own_ref.shape[0]):
        for place, ref, which in ((own_place, own_ref, core), (sib_place, sib_ref, 1 - core)):
            row = pl.multiple_of(2 * part * k + part * which, 16)
            ref[place[k]] = full_ref[pl.ds(row, part), :].astype(BF)


def deal(full, part, dp_size, core, own_place, sib_place):
    shape = jax.ShapeDtypeStruct((dp_size, part, full.shape[1]), BF)
    return pl.pallas_call(
        functools.partial(deal_kernel, part),
        in_specs=[pl.BlockSpec(memory_space=pltpu.SMEM)] * 3 + [pl.BlockSpec(memory_space=pltpu.VMEM)],
        out_shape=[shape, shape],
        compiler_params=params(),
        name="deal",
    )(core, own_place, sib_place, full)


def gather_weights(qkv_weight, out_weight, router, norm_params, sizes, ids, tables):
    dp_size, tensor_size = sizes
    dp_index, _, core = ids
    rows = qkv_weight.shape[1]
    columns = qkv_weight.shape[2]
    width = rows * dp_size
    half = width // 2
    part = rows // 2
    turned = jnp.concatenate([qkv_weight, out_weight.T[None]], axis=0)
    turned = turned.transpose(1, 0, 2).reshape(rows, 4 * columns)
    small = jnp.concatenate(
        [jnp.pad(norm_params, ((0, 0), (0, 4 * columns - rows))), jnp.pad(router.T, ((0, 0), (0, 3 * columns)))],
        axis=0,
    )
    packed = jnp.concatenate([turned, jnp.pad(small, ((0, 14), (0, 0)))], axis=0)
    spread = lax.all_gather(packed, "tensor", axis=0)
    norm_cols = spread[:, rows, :rows]
    router_row = spread[:, rows + 1, :columns].reshape(1, width)
    by_kind = spread[:, :rows].reshape(tensor_size, rows, 4, columns)
    by_kind = lax.dynamic_slice_in_dim(by_kind, core * part, part, axis=1)
    by_kind = by_kind.transpose(1, 2, 0, 3).reshape(part, 4, width)
    one = by_kind[:, :3, :half].reshape(part, 3 * half)
    two = by_kind[:, :3, half:].reshape(part, 3 * half)
    out_rows = by_kind[:, 3]
    experts = dp_size * router.shape[1]
    extra_rows = -(-(4 + experts) // 16) * 16
    extra = jnp.zeros((extra_rows, 3 * half), BF)
    extra = lax.dynamic_update_slice(extra, norm_cols, (0, dp_index * rows))
    extra = lax.dynamic_update_slice(extra, router_row, (4 + dp_index, 0))
    got_one = gather_steps(jnp.concatenate([one, extra], axis=0), dp_size, tensor_size)
    sib_one = swap(got_one, dp_size, tensor_size, 0, 1)
    smalls = jnp.sum(got_one[:, part:, :width].astype(F32), axis=0)
    got_two = gather_steps(two, dp_size, tensor_size)
    sib_two = swap(got_two, dp_size, tensor_size, 0, 1)
    got_out = gather_steps(out_rows, dp_size, tensor_size)
    sib_out = swap(got_out, dp_size, tensor_size, 0, 1)
    weight_one = assemble(got_one, sib_one, part, *tables)
    weight_two = assemble(got_two, sib_two, part, *tables)
    out_w = assemble(got_out, sib_out, part, *tables)
    return weight_one, weight_two, out_w, smalls[:4], smalls[4 : 4 + experts].astype(BF)


def gather_weights_plain(qkv_weight, out_weight, router, norm_params):
    qkv = lax.all_gather(qkv_weight, "dp", axis=1, tiled=True)
    qkv = lax.all_gather(qkv, "tensor", axis=2, tiled=True)
    out_w, router, norms = (
        lax.all_gather(lax.all_gather(w, "dp", axis=1, tiled=True), "tensor", axis=0, tiled=True)
        for w in (out_weight, router, norm_params)
    )
    width = qkv.shape[1]
    half = width // 2
    one = qkv[:, :, :half].transpose(1, 0, 2).reshape(width, 3 * half)
    two = qkv[:, :, half:].transpose(1, 0, 2).reshape(width, 3 * half)
    return one, two, out_w.T, norms.astype(F32), router.T


def scatter_weight(full, part, sizes, tables):
    dp_size, tensor_size = sizes
    own, sib = deal(full, part, dp_size, *tables)
    got = swap(sib, dp_size, tensor_size, 0, 1)
    return scatter_steps((own.astype(F32) + got.astype(F32)).astype(BF), dp_size, tensor_size)


def sum_small(values, sizes):
    dp_size, tensor_size = sizes
    mask = 1
    while mask < tensor_size:
        values = values + swap(values, dp_size, tensor_size, 0, mask)
        mask *= 2
    mask = 1
    while mask < dp_size:
        values = values + swap(values, dp_size, tensor_size, mask, 0)
        mask *= 2
    return values


def pad_images(rows):
    images = rows.shape[0] // SEQ
    return jnp.pad(rows.reshape(images, SEQ, -1), ((0, 0), (0, PAD - SEQ), (0, 0)))


def trim_images(padded):
    return padded[:, :SEQ].reshape(-1, padded.shape[2])


def on_device(
    sizes, tokens, qkv_weight, out_weight, router, norm_params, expert_in, expert_out, cotangent
):
    dp_size, tensor_size = sizes
    dp_index = lax.axis_index("dp")
    tensor_index = lax.axis_index("tensor")
    core = tensor_index % 2
    high = tensor_index // 2
    width = tokens.shape[1]
    half = width // 2
    rows = qkv_weight.shape[1]
    columns = qkv_weight.shape[2]
    part = rows // 2
    stepwise = rows % 32 == 0
    x_img = pad_images(tokens)
    g_img = pad_images(cotangent)
    if stepwise:
        tables = (core.reshape(1).astype(jnp.int32),) + places(dp_size, dp_index, core)
        weight_one, weight_two, out_w, norms, router_t = gather_weights(
            qkv_weight, out_weight, router, norm_params, sizes, (dp_index, tensor_index, core), tables
        )
    else:
        weight_one, weight_two, out_w, norms, router_t = gather_weights_plain(
            qkv_weight, out_weight, router, norm_params
        )
    experts = router_t.shape[0]
    normed = first_norm(x_img, norms)
    qkv_one, mixed_one, probs_one = attend(normed, weight_one)
    qkv_two, mixed_two, probs_two = attend(normed, weight_two)
    y, logits, outgoing = route(x_img, mixed_one, mixed_two, out_w, norms, router_t, g_img)

    outgoing = outgoing.reshape(experts, SLOT_ROWS, width)
    arrived = lax.all_to_all(outgoing, "dp", split_axis=0, concat_axis=0, tiled=True)
    across = swap(arrived, dp_size, tensor_size, 0, 2)
    pair = jnp.concatenate([arrived, across], axis=0)
    near = swap(pair, dp_size, tensor_size, 0, 1)
    keep, away, first_grad, second_grad = run_expert(pair, near, expert_in[0], expert_out[0])
    got = swap(away, dp_size, tensor_size, 0, 1)
    summed = (keep.astype(F32) + got.astype(F32)).astype(BF)
    got = swap(summed[dp_size:], dp_size, tensor_size, 0, 2)
    summed = (summed[:dp_size].astype(F32) + got.astype(F32)).astype(BF)
    back = lax.all_to_all(summed, "dp", split_axis=0, concat_axis=0, tiled=True)
    back = back.reshape(experts * SLOT_ROWS, width)

    out_img, grad_y, grad_mixed, out_grad_t, small_two = moe_back(
        y, g_img, logits, back, norms, router_t, out_w, mixed_one, mixed_two
    )
    grads_one, dw_one = attend_back(normed, qkv_one, probs_one, mixed_one, grad_mixed, 0)
    grads_two, dw_two = attend_back(normed, qkv_two, probs_two, mixed_two, grad_mixed, 1)
    in_img, small_one = input_back(
        x_img, grad_y, grads_one, grads_two, weight_one, weight_two, norms
    )
    small = sum_small(
        jnp.concatenate([small_one[0:2], small_two[0:2], small_two[8:]], axis=0), sizes
    )
    norm_grad = lax.dynamic_slice(small, (tensor_index, dp_index * rows), (1, rows))
    router_grad = lax.dynamic_slice(
        small, (4 + dp_index, tensor_index * columns), (1, columns)
    ).reshape(columns, 1)

    if stepwise:
        one = scatter_weight(dw_one, part, sizes, tables).reshape(part, 3, half)
        two = scatter_weight(dw_two, part, sizes, tables).reshape(part, 3, half)
        out_t = scatter_weight(out_grad_t, part, sizes, tables).reshape(part, 2, half)
        stacked = jnp.stack(
            [jnp.concatenate([one, out_t[:, :1]], axis=1), jnp.concatenate([two, out_t[:, 1:]], axis=1)]
        )
        mine = jnp.where(high == 0, stacked[0], stacked[1])
        other = jnp.where(high == 0, stacked[1], stacked[0])
        got = swap(other, dp_size, tensor_size, 0, 2)
        total = (mine.astype(F32) + got.astype(F32)).reshape(part, 4, 2, columns)
        keep = jnp.where(core == 0, total[:, :, 0], total[:, :, 1])
        give = jnp.where(core == 0, total[:, :, 1], total[:, :, 0])
        got = swap(give, dp_size, tensor_size, 0, 1)
        top = jnp.where(core == 0, keep, got)
        bottom = jnp.where(core == 0, got, keep)
        both = jnp.concatenate([top, bottom], axis=0).transpose(1, 0, 2)
        qkv_grad = both[:3]
        out_grad = both[3].T
    else:
        full = jnp.concatenate(
            [dw_one.reshape(width, 3, half), dw_two.reshape(width, 3, half)], axis=2
        ).transpose(1, 0, 2)
        qkv_grad = lax.psum_scatter(full, "dp", scatter_dimension=1, tiled=True)
        qkv_grad = lax.psum_scatter(qkv_grad, "tensor", scatter_dimension=2, tiled=True)
        out_grad = lax.psum_scatter(out_grad_t.T, "dp", scatter_dimension=1, tiled=True)
        out_grad = lax.psum_scatter(out_grad, "tensor", scatter_dimension=0, tiled=True)
    return (
        trim_images(out_img),
        trim_images(in_img),
        qkv_grad,
        out_grad,
        router_grad,
        norm_grad,
        first_grad[None],
        second_grad[None],
    )


def solution(mesh):
    sizes = (mesh.shape["dp"], mesh.shape["tensor"])
    return jax.shard_map(
        functools.partial(on_device, sizes),
        mesh=mesh,
        in_specs=(
            P(("dp", "tensor"), None),
            P(None, "dp", "tensor"),
            P("tensor", "dp"),
            P("tensor", "dp"),
            P("tensor", "dp"),
            P("dp", None, "tensor"),
            P("dp", "tensor", None),
            P(("dp", "tensor"), None),
        ),
        out_specs=(
            P(("dp", "tensor"), None),
            P(("dp", "tensor"), None),
            P(None, "dp", "tensor"),
            P("tensor", "dp"),
            P("tensor", "dp"),
            P("tensor", "dp"),
            P("dp", None, "tensor"),
            P("dp", "tensor", None),
        ),
        check_vma=False,
    )
```

time: 919 us -> 326 us (0.35)
  blocking collectives: 289 us -> 33.9 us
  matrix products: 181 us -> 0 us
  local copies, waits for them, and re-layouts: 199 us -> 31.5 us
  Pallas kernels: 0 us -> 135 us
  waiting for transfers between devices: 139 us -> 82.7 us
  other arithmetic: 63.1 us -> 7.83 us
  between operations: 16.8 us -> 1.25 us
  starting transfers between devices: 20.8 us -> 32.9 us
    unnamed x5 -> x0, blocking collectives: 178 us -> none
    dot_general x75 -> x0, matrix products: 167 us -> none  [the longest x1 18.3 us: on_device(): jnp.einsum('krc,kdc->rd', grad_proj, qkv_use, preferred_element_type=jnp....]
    pallas_call x0 -> x15, Pallas kernels: none -> 135 us  [the longest x2 36 us: attend_back(): pl.pallas_call(functools.partial(attend_back_kernel, span // 128), grid=(...]
    all_gather x7 -> x1, blocking collectives: 111 us -> 9.54 us  [gather_weights(): spread = lax.all_gather(packed, 'tensor', axis=0)]
    ppermute x0 -> x35, waiting for transfers between devices: none -> 82.7 us  [the longest x9 35 us: gather_steps(): got = lax.ppermute(held, AXES, step_pairs(dp_size, tensor_size, step))]
    unnamed x14 -> x0, waiting for transfers between devices: 77.1 us -> none
    unnamed x115 -> x22, local copies, waits for them, and re-layouts: 53.9 us -> 4.05 us
    while x8 -> x0, local copies, waits for them, and re-layouts: 36.3 us -> none  [the longest x4 20 us: attention_forward(): lax.map(lambda pieces: attend_forward(pieces[0], pieces[1], pieces[2], sc...]
  transfers between devices with their start and end apart: 14 -> 35, of which waited for: 7 -> 20; matrix products, arithmetic and copies ran while one was open for 19% -> 10% of each run, Pallas kernels for 0% -> 24%
where the time goes in v1:
time: 326 us; the launch traced here: 325 us
  Pallas kernels  135 us (41%)
  waiting for transfers between devices  82.7 us (25%)
  blocking collectives  33.9 us (10%)
  starting transfers between devices  32.9 us (10%)
  local copies, waits for them, and re-layouts  31.5 us (10%)
  other arithmetic  7.83 us (2%)
    pallas_call x2, Pallas kernels, attend_back(): pl.pallas_call(functools.partial(attend_back_kernel, span // 128), grid=(...  36 us
    ppermute x9, waiting for transfers between devices, gather_steps(): got = lax.ppermute(held, AXES, step_pairs(dp_size, tensor_size, step))  35 us
    pallas_call x2, Pallas kernels, attend(): pl.pallas_call(functools.partial(attend_kernel, span // 128), grid=(image...  26.3 us
    ppermute x17, waiting for transfers between devices, swap(): return lax.ppermute(value, AXES, pairs)  24.4 us
    ppermute x9, waiting for transfers between devices, scatter_steps(): lax.ppermute(held[half:], AXES, step_pairs(dp_size, tensor_size, step))  23.3 us
    pallas_call x1, Pallas kernels, moe_back(): pl.pallas_call(functools.partial(moe_back_kernel, half), grid=(images,),...  17 us
    pallas_call x1, Pallas kernels, route(): pl.pallas_call(functools.partial(route_kernel, half), grid=(images,), in_...  13.2 us
    all_to_all x1, blocking collectives, on_device(): lax.all_to_all(outgoing, 'dp', split_axis=0, concat_axis=0, tiled=True)  12.8 us
  transfers between devices with their start and end apart: 35, of which 20 were waited for; matrix products, arithmetic and copies ran while one was open for 10% of the time, Pallas kernels for 24%

profile of v1, /device:TPU:0, one launch (start us, length us, event | category | flops | bytes accessed | tf_op | source)
XLA Modules:
  0.0 324.7 jit_solution(9776645477649733795)
XLA Ops:
  3.6 9.5 %all-gather = bf16[448,768]{1,0:T(8,128)(2,1)S(1)} all-gather(bf16[112,768]{1,0:T(8,128)(2,1)S(1)} %fusion.2), channel_id=2, replica_groups=mesh['dp'=8,'tensor'=4] {'tensor'}, dimensions={0}, use_global_device_ids=true | all-gather | bytes 860160 | tf_op jit(solution)/shard_map/all_gather | solution.py:562
  22.0 14.1 %collective-permute-done = bf16[1,64,1152]{2,1,0:T(8,128)(2,1)S(1)} collective-permute-done((bf16[1,64,1152]{2,1,0:T(8,128)(2,1)S(1)}, bf16[1,64,1152]{2,1,0:T(8,128)(2,1)S(1)}, u32[]{:S(2)}, u32[]{:S(2)}) %collective-permute-start) | collective-permute-done | bytes 147488 | tf_op jit(solution)/shard_map/ppermute | solution.py:496
  38.5 9.6 %collective-permute-done.1 = bf16[2,64,1152]{2,1,0:T(8,128)(2,1)S(1)} collective-permute-done((bf16[2,64,1152]{2,1,0:T(8,128)(2,1)S(1)}, bf16[2,64,1152]{2,1,0:T(8,128)(2,1)S(1)}, u32[]{:S(2)}, u32[]{:S(2)}) %collective-permute-start.1) | collective-permute-done | bytes 294944 | tf_op jit(solution)/shard_map/ppermute | solution.py:496
  52.8 3.1 collective-permute-done.5
  59.2 6.8 %collective-permute-done.6 = bf16[4,48,1152]{2,1,0:T(8,128)(2,1)S(1)} collective-permute-done((bf16[4,48,1152]{2,1,0:T(8,128)(2,1)S(1)}, bf16[4,48,1152]{2,1,0:T(8,128)(2,1)S(1)}, u32[]{:S(2)}, u32[]{:S(2)}) %collective-permute-start.6) | collective-permute-done | bytes 442400 | tf_op jit(solution)/shard_map/ppermute | solution.py:496
  76.8 5.4 %first_norm.1.n_ref = bf16[6,208,768]{2,1,0:T(8,128)(2,1)} custom-call(bf16[6,208,768]{2,1,0:T(8,128)(2,1)} %pad.19.x_ref, f32[4,768]{1,0:T(4,128)} %slice.168.norms_ref), custom_call_target="tpu_custom_call" | custom-call | tf_op jit(solution)/shard_map/first_norm/pallas_call | solution.py:62
  84.6 2.8 assemble.4.w_ref.w2_ref
  87.4 13.2 %attend.3 = (bf16[6,208,1152]{2,1,0:T(8,128)(2,1)}, bf16[6,208,384]{2,1,0:T(8,128)(2,1)}, bf16[6,6,208,208]{3,2,1,0:T(8,128)(2,1)}) custom-call(bf16[6,208,768]{2,1,0:T(8,128)(2,1)} %first_norm.1.n_ref, bf16[768,1152]{1,0:T(8,128)(2,1)} %assemble.4.w_ref.w2_ref), custom_call_target="tpu_custom_call" | custom-call | tf_op jit(solution)/shard_map/attend/pallas_call | solution.py:106
  100.5 3.0 assemble.3.w_ref.w1_ref
  103.5 13.2 %attend.2 = (bf16[6,208,1152]{2,1,0:T(8,128)(2,1)}, bf16[6,208,384]{2,1,0:T(8,128)(2,1)}, bf16[6,6,208,208]{3,2,1,0:T(8,128)(2,1)}) custom-call(bf16[6,208,768]{2,1,0:T(8,128)(2,1)} %first_norm.1.n_ref, bf16[768,1152]{1,0:T(8,128)(2,1)} %assemble.3.w_ref.w1_ref), custom_call_target="tpu_custom_call" | custom-call | tf_op jit(solution)/shard_map/attend/pallas_call | solution.py:106
  116.7 13.2 %route.1 = (f32[6,208,768]{2,1,0:T(8,128)}, f32[6,8,208]{2,1,0:T(8,128)}, bf16[128,768]{1,0:T(8,128)(2,1)}) custom-call(bf16[6,208,768]{2,1,0:T(8,128)(2,1)} %pad.19.x_ref, bf16[6,208,384]{2,1,0:T(8,128)(2,1)} %get-tuple-element.38.m1_ref.mixed_ref, bf16[6,208,384]{2,1,0:T(8,128)(2,1)} %get-tuple-element.39.m2_ref.mixed_ref, ...), custom_call_target="tpu_custom_call" | custom-call | tf_op jit(solution)/shard_map/route/pallas_call | solution.py:182
  129.9 12.8 %all_to_all.10 = bf16[8,16,768]{2,1,0:T(8,128)(2,1)S(1)} all-to-all(bf16[8,16,768]{2,1,0:T(8,128)(2,1)} %bitcast.57), channel_id=1, replica_groups=mesh['dp'=8,'tensor'=4] {'dp'}, dimensions={0} | all-to-all | bytes 393216 | tf_op jit(solution)/shard_map/all_to_all | solution.py:664
  143.9 4.6 %collective-permute-done.12 = bf16[8,16,768]{2,1,0:T(8,128)(2,1)S(1)} collective-permute-done((bf16[8,16,768]{2,1,0:T(8,128)(2,1)S(1)}, bf16[8,16,768]{2,1,0:T(8,128)(2,1)S(1)}, u32[]{:S(2)}, u32[]{:S(2)}) %collective-permute-start.12) | collective-permute-done | bytes 196640 | tf_op jit(solution)/shard_map/ppermute | solution.py:464
  151.0 5.9 %expert.1 = (bf16[16,16,768]{2,1,0:T(8,128)(2,1)}, bf16[16,16,768]{2,1,0:T(8,128)(2,1)}, f32[768,768]{1,0:T(8,128)}, f32[768,768]{1,0:T(8,128)}) custom-call(bf16[16,16,768]{2,1,0:T(8,128)(2,1)} %copy-done.1, bf16[16,16,768]{2,1,0:T(8,128)(2,1)} %copy-done.5, bf16[768,768]{1,0:T(8,128)(2,1)} %bitcast.52, bf16[768,768]{1,0:T(8,128)(2,1)} %bitcast.53), custom_call_target="tpu_custom_call" | custom-call | tf_op jit(solution)/shard_map/expert/pallas_call | solution.py:248
  161.2 5.8 %collective-permute-done.15 = bf16[8,16,768]{2,1,0:T(8,128)(2,1)S(1)} collective-permute-done((bf16[8,16,768]{2,1,0:T(8,128)(2,1)S(1)}, bf16[8,16,768]{2,1,0:T(8,128)(2,1)S(1)}, u32[]{:S(2)}, u32[]{:S(2)}) %collective-permute-start.15) | collective-permute-done | bytes 196640 | tf_op jit(solution)/shard_map/ppermute | solution.py:464
  167.1 11.6 %all_to_all.11 = bf16[8,16,768]{2,1,0:T(8,128)(2,1)} all-to-all(bf16[8,16,768]{2,1,0:T(8,128)(2,1)S(1)} %add_convert_fusion.9), channel_id=1, replica_groups=mesh['dp'=8,'tensor'=4] {'dp'}, dimensions={0} | all-to-all | bytes 393216 | tf_op jit(solution)/shard_map/all_to_all | solution.py:673
  178.6 17.0 %moe_back.1 = (bf16[6,208,768]{2,1,0:T(8,128)(2,1)}, f32[6,208,768]{2,1,0:T(8,128)}, bf16[6,208,768]{2,1,0:T(8,128)(2,1)}, f32[768,768]{1,0:T(8,128)}, f32[16,768]{1,0:T(8,128)}) custom-call(f32[6,208,768]{2,1,0:T(8,128)} %get-tuple-element.40.y_ref, bf16[6,208,768]{2,1,0:T(8,128)(2,1)} %pad.23.g_ref, f32[6,8,208]{2,1,0:T(8,128)} %get-tuple-element.41.logits_ref, ...), custom_call_target="tpu_custom_call" | custom-call | tf_op jit(solution)/shard_map/moe_back/pallas_call | solution.py:324
  195.7 2.8 deal.4
  198.5 18.0 %attend_back.3 = (bf16[6,208,1152]{2,1,0:T(8,128)(2,1)}, f32[768,1152]{1,0:T(8,128)}) custom-call(bf16[6,208,768]{2,1,0:T(8,128)(2,1)} %first_norm.1.n_ref, bf16[6,208,1152]{2,1,0:T(8,128)(2,1)} %get-tuple-element.51.qkv_ref, bf16[6,6,208,208]{3,2,1,0:T(8,128)(2,1)} %get-tuple-element.52.probs_ref, bf16[6,208,384]{2,1,0:T(8,128)(2,1)} %get-tuple-element.39.m2_ref.mixed_ref, ...), custom_call_target="tpu_custom_call" | custom-call | tf_op jit(solution)/shard_map/attend_back/pallas_call | solution.py:397
  216.5 3.5 %deal.5 = (bf16[8,48,1152]{2,1,0:T(8,128)(2,1)}, bf16[8,48,1152]{2,1,0:T(8,128)(2,1)}) custom-call(s32[1]{0:T(128)} %bitcast.8.core_ref, s32[8]{0:T(128)} %get-tuple-element.102.own_place, s32[8]{0:T(128)} %get-tuple-element.101.sib_place, f32[768,1152]{1,0:T(8,128)} %get-tuple-element.61.full_ref), custom_call_target="tpu_custom_call" | custom-call | tf_op jit(solution)/shard_map/deal/pallas_call | solution.py:538
  221.7 18.0 %attend_back.2 = (bf16[6,208,1152]{2,1,0:T(8,128)(2,1)}, f32[768,1152]{1,0:T(8,128)}) custom-call(bf16[6,208,768]{2,1,0:T(8,128)(2,1)} %first_norm.1.n_ref, bf16[6,208,1152]{2,1,0:T(8,128)(2,1)} %get-tuple-element.47.qkv_ref, bf16[6,6,208,208]{3,2,1,0:T(8,128)(2,1)} %get-tuple-element.48.probs_ref, bf16[6,208,384]{2,1,0:T(8,128)(2,1)} %get-tuple-element.38.m1_ref.mixed_ref, ...), custom_call_target="tpu_custom_call" | custom-call | tf_op jit(solution)/shard_map/attend_back/pallas_call | solution.py:397
  239.7 12.7 %input_back.1 = (f32[6,208,768]{2,1,0:T(8,128)}, f32[8,768]{1,0:T(8,128)}) custom-call(bf16[6,208,768]{2,1,0:T(8,128)(2,1)} %pad.19.x_ref, f32[6,208,768]{2,1,0:T(8,128)} %get-tuple-element.46.gy_ref, bf16[6,208,1152]{2,1,0:T(8,128)(2,1)} %get-tuple-element.50.p1_ref, bf16[6,208,1152]{2,1,0:T(8,128)(2,1)} %get-tuple-element.53.p2_ref, ...), custom_call_target="tpu_custom_call" | custom-call | tf_op jit(solution)/shard_map/input_back/pallas_call | solution.py:436
  253.3 3.5 %deal.3 = (bf16[8,48,1152]{2,1,0:T(8,128)(2,1)}, bf16[8,48,1152]{2,1,0:T(8,128)(2,1)}) custom-call(s32[1]{0:T(128)} %bitcast.8.core_ref, s32[8]{0:T(128)} %get-tuple-element.102.own_place, s32[8]{0:T(128)} %get-tuple-element.101.sib_place, f32[768,1152]{1,0:T(8,128)} %get-tuple-element.55.full_ref), custom_call_target="tpu_custom_call" | custom-call | tf_op jit(solution)/shard_map/deal/pallas_call | solution.py:538
  259.0 6.7 %collective-permute-done.22 = bf16[2,48,768]{2,1,0:T(8,128)(2,1)S(1)} collective-permute-done((bf16[2,48,768]{2,1,0:T(8,128)(2,1)S(1)}, bf16[2,48,768]{2,1,0:T(8,128)(2,1)S(1)}, u32[]{:S(2)}, u32[]{:S(2)}) %collective-permute-start.22) | collective-permute-done | bytes 147488 | tf_op jit(solution)/shard_map/ppermute | solution.py:505
  267.3 4.2 %collective-permute-done.23 = bf16[1,48,768]{2,1,0:T(8,128)(2,1)S(1)} collective-permute-done((bf16[1,48,768]{2,1,0:T(8,128)(2,1)S(1)}, bf16[1,48,768]{2,1,0:T(8,128)(2,1)S(1)}, u32[]{:S(2)}, u32[]{:S(2)}) %collective-permute-start.23) | collective-permute-done | bytes 73760 | tf_op jit(solution)/shard_map/ppermute | solution.py:505
  279.1 3.8 %collective-permute-done.18 = bf16[2,48,1152]{2,1,0:T(8,128)(2,1)S(1)} collective-permute-done((bf16[2,48,1152]{2,1,0:T(8,128)(2,1)S(1)}, bf16[2,48,1152]{2,1,0:T(8,128)(2,1)S(1)}, u32[]{:S(2)}, u32[]{:S(2)}) %collective-permute-start.18) | collective-permute-done | bytes 221216 | tf_op jit(solution)/shard_map/ppermute | solution.py:505
  283.0 4.0 %collective-permute-start.19 = (bf16[1,48,1152]{2,1,0:T(8,128)(2,1)S(1)}, bf16[1,48,1152]{2,1,0:T(8,128)(2,1)S(1)}, u32[]{:S(2)}, u32[]{:S(2)}) collective-permute-start(bf16[1,48,1152]{2,1,0:T(8,128)(2,1)S(1)} %slice.179), channel_id=1, source_target_pairs={{0,16},{1,5},{2,18},{3,7},{4,20},{5,1},{6,22},{7,3},{8,24},{9,13},... | collective-permute-start | bytes 331784 | tf_op jit(solution)/shard_map/ppermute | solution.py:505
  293.3 3.6 %collective-permute-done.31 = f32[12,768]{1,0:T(8,128)S(1)} collective-permute-done((f32[12,768]{1,0:T(8,128)S(1)}, f32[12,768]{1,0:T(8,128)S(1)}, u32[]{:S(2)}, u32[]{:S(2)}) %collective-permute-start.31) | collective-permute-done | bytes 36896 | tf_op jit(solution)/shard_map/ppermute | solution.py:464
  301.1 4.4 %collective-permute-done.33 = f32[12,768]{1,0:T(8,128)S(1)} collective-permute-done((f32[12,768]{1,0:T(8,128)S(1)}, f32[12,768]{1,0:T(8,128)S(1)}, u32[]{:S(2)}, u32[]{:S(2)}) %collective-permute-start.33) | collective-permute-done | bytes 36896 | tf_op jit(solution)/shard_map/ppermute | solution.py:464
  305.5 3.5 %collective-permute-start.34 = (f32[12,768]{1,0:T(8,128)S(1)}, f32[12,768]{1,0:T(8,128)S(1)}, u32[]{:S(2)}, u32[]{:S(2)}) collective-permute-start(f32[12,768]{1,0:T(8,128)S(1)} %add.127), channel_id=1, source_target_pairs={{0,16},{1,17},{2,18},{3,19},{4,20},{5,21},{6,22},{7,23},{8,24},{9,... | collective-permute-start | bytes 110600 | tf_op jit(solution)/shard_map/ppermute | solution.py:464
  313.4 4.1 %slice.135 = f32[6,197,768]{2,1,0:T(8,128)} slice(f32[6,208,768]{2,1,0:T(8,128)} %get-tuple-element.54), slice={[0:6], [0:197], [0:768]} | slice | bytes 7262208 | tf_op jit(solution)/shard_map/slice | solution.py:629
  317.5 4.3 %reshape.69 = f32[1182,768]{1,0:T(8,128)} reshape(f32[6,197,768]{2,1,0:T(8,128)} %slice.135) | data formatting | bytes 7262208 | tf_op jit(solution)/shard_map/reshape | solution.py:629
  (170 shorter events, 74.7 us)
Async XLA Ops:
  14.7 21.6 %collective-permute-start.8 = (bf16[1,48,768]{2,1,0:T(8,128)(2,1)S(1)}, bf16[1,48,768]{2,1,0:T(8,128)(2,1)S(1)}, u32[]{:S(2)}, u32[]{:S(2)}) collective-permute-start(bf16[1,48,768]{2,1,0:T(8,128)(2,1)S(1)} %slice_bitcast_fusion.2), channel_id=1, source_target_pairs={{0,16},{1,5},{2,18},{3,7},{4,20},{5,1},{6,22},{7,3},{8,24},{9,13},... | collective-permute-start | bytes 221192 | tf_op jit(solution)/shard_map/ppermute | solution.py:496
  17.5 20.8 %collective-permute-start.4 = (bf16[1,48,1152]{2,1,0:T(8,128)(2,1)S(1)}, bf16[1,48,1152]{2,1,0:T(8,128)(2,1)S(1)}, u32[]{:S(2)}, u32[]{:S(2)}) collective-permute-start(bf16[1,48,1152]{2,1,0:T(8,128)(2,1)S(1)} %broadcast_in_dim_reshape.3), channel_id=1, source_target_pairs={{0,16},{1,5},{2,18},{3,7},{4,20},{5,1},{6,22},{7,3},{8,24},{9,13},... | collective-permute-start | bytes 331784 | tf_op jit(solution)/shard_map/ppermute | solution.py:496
  18.7 17.4 %collective-permute-start = (bf16[1,64,1152]{2,1,0:T(8,128)(2,1)S(1)}, bf16[1,64,1152]{2,1,0:T(8,128)(2,1)S(1)}, u32[]{:S(2)}, u32[]{:S(2)}) collective-permute-start(bf16[1,64,1152]{2,1,0:T(8,128)(2,1)S(1)} %maximum_bitcast_fusion.2), channel_id=1, source_target_pairs={{0,16},{1,5},{2,18},{3,7},{4,20},{5,1},{6,22},{7,3},{8,24},{9,13},... | collective-permute-start | bytes 442376 | tf_op jit(solution)/shard_map/ppermute | solution.py:496
  36.2 11.9 %collective-permute-start.1 = (bf16[2,64,1152]{2,1,0:T(8,128)(2,1)S(1)}, bf16[2,64,1152]{2,1,0:T(8,128)(2,1)S(1)}, u32[]{:S(2)}, u32[]{:S(2)}) collective-permute-start(bf16[2,64,1152]{2,1,0:T(8,128)(2,1)S(1)} %pad_maximum_fusion.4), channel_id=1, source_target_pairs={{0,8},{1,17},{2,10},{3,19},{4,12},{5,21},{6,14},{7,23},{8,0},{9,25... | collective-permute-start | bytes 884744 | tf_op jit(solution)/shard_map/ppermute | solution.py:496
  36.3 14.9 %collective-permute-start.9 = (bf16[2,48,768]{2,1,0:T(8,128)(2,1)S(1)}, bf16[2,48,768]{2,1,0:T(8,128)(2,1)S(1)}, u32[]{:S(2)}, u32[]{:S(2)}) collective-permute-start(bf16[2,48,768]{2,1,0:T(8,128)(2,1)S(1)} %pad_maximum_fusion.7), channel_id=1, source_target_pairs={{0,8},{1,17},{2,10},{3,19},{4,12},{5,21},{6,14},{7,23},{8,0},{9,25... | collective-permute-start | bytes 442376 | tf_op jit(solution)/shard_map/ppermute | solution.py:496
  38.4 17.6 %collective-permute-start.5 = (bf16[2,48,1152]{2,1,0:T(8,128)(2,1)S(1)}, bf16[2,48,1152]{2,1,0:T(8,128)(2,1)S(1)}, u32[]{:S(2)}, u32[]{:S(2)}) collective-permute-start(bf16[2,48,1152]{2,1,0:T(8,128)(2,1)S(1)} %pad_maximum_fusion.6), channel_id=1, source_target_pairs={{0,8},{1,17},{2,10},{3,19},{4,12},{5,21},{6,14},{7,23},{8,0},{9,25... | collective-permute-start | bytes 663560 | tf_op jit(solution)/shard_map/ppermute | solution.py:496
  48.1 9.9 %collective-permute-start.2 = (bf16[4,64,1152]{2,1,0:T(8,128)(2,1)S(1)}, bf16[4,64,1152]{2,1,0:T(8,128)(2,1)S(1)}, u32[]{:S(2)}, u32[]{:S(2)}) collective-permute-start(bf16[4,64,1152]{2,1,0:T(8,128)(2,1)S(1)} %pad_maximum_fusion.1), channel_id=1, source_target_pairs={{0,4},{1,9},{2,6},{3,11},{4,0},{5,13},{6,2},{7,15},{8,12},{9,1},{1... | collective-permute-start | bytes 1769480 | tf_op jit(solution)/shard_map/ppermute | solution.py:496
  51.2 15.5 %collective-permute-start.10 = (bf16[4,48,768]{2,1,0:T(8,128)(2,1)S(1)}, bf16[4,48,768]{2,1,0:T(8,128)(2,1)S(1)}, u32[]{:S(2)}, u32[]{:S(2)}) collective-permute-start(bf16[4,48,768]{2,1,0:T(8,128)(2,1)S(1)} %pad_maximum_fusion.5), channel_id=1, source_target_pairs={{0,4},{1,9},{2,6},{3,11},{4,0},{5,13},{6,2},{7,15},{8,12},{9,1},{1... | collective-permute-start | bytes 884744 | tf_op jit(solution)/shard_map/ppermute | solution.py:496
  56.0 10.0 %collective-permute-start.6 = (bf16[4,48,1152]{2,1,0:T(8,128)(2,1)S(1)}, bf16[4,48,1152]{2,1,0:T(8,128)(2,1)S(1)}, u32[]{:S(2)}, u32[]{:S(2)}) collective-permute-start(bf16[4,48,1152]{2,1,0:T(8,128)(2,1)S(1)} %pad_maximum_fusion.3), channel_id=1, source_target_pairs={{0,4},{1,9},{2,6},{3,11},{4,0},{5,13},{6,2},{7,15},{8,12},{9,1},{1... | collective-permute-start | bytes 1327112 | tf_op jit(solution)/shard_map/ppermute | solution.py:496
  58.2 42.3 %collective-permute-start.3 = (bf16[8,64,1152]{2,1,0:T(8,128)(2,1)S(1)}, bf16[8,64,1152]{2,1,0:T(8,128)(2,1)}, u32[]{:S(2)}, u32[]{:S(2)}) collective-permute-start(bf16[8,64,1152]{2,1,0:T(8,128)(2,1)S(1)} %pad_maximum_fusion.own_ref), channel_id=1, source_target_pairs={{0,1},{1,0},{2,3},{3,2},{4,5},{5,4},{6,7},{7,6},{8,9},{9,8},{10,11... | collective-permute-start | bytes 3538952 | tf_op jit(solution)/shard_map/ppermute | solution.py:464
  66.8 17.8 %collective-permute-start.7 = (bf16[8,48,1152]{2,1,0:T(8,128)(2,1)}, bf16[8,48,1152]{2,1,0:T(8,128)(2,1)}, u32[]{:S(2)}, u32[]{:S(2)}) collective-permute-start(bf16[8,48,1152]{2,1,0:T(8,128)(2,1)} %constant_dynamic-update-slice_fusion.own_ref), channel_id=1, source_target_pairs={{0,1},{1,0},{2,3},{3,2},{4,5},{5,4},{6,7},{7,6},{8,9},{9,8},{10,11... | collective-permute-start | bytes 2654216 | tf_op jit(solution)/shard_map/ppermute | solution.py:464
  67.7 14.6 %collective-permute-start.11 = (bf16[8,48,768]{2,1,0:T(8,128)(2,1)}, bf16[8,48,768]{2,1,0:T(8,128)(2,1)}, u32[]{:S(2)}, u32[]{:S(2)}) collective-permute-start(bf16[8,48,768]{2,1,0:T(8,128)(2,1)} %pad_maximum_fusion.2.own_ref), channel_id=1, source_target_pairs={{0,1},{1,0},{2,3},{3,2},{4,5},{5,4},{6,7},{7,6},{8,9},{9,8},{10,11... | collective-permute-start | bytes 1769480 | tf_op jit(solution)/shard_map/ppermute | solution.py:464
  142.8 5.7 %collective-permute-start.12 = (bf16[8,16,768]{2,1,0:T(8,128)(2,1)S(1)}, bf16[8,16,768]{2,1,0:T(8,128)(2,1)S(1)}, u32[]{:S(2)}, u32[]{:S(2)}) collective-permute-start(bf16[8,16,768]{2,1,0:T(8,128)(2,1)S(1)} %all_to_all.10), channel_id=1, source_target_pairs={{0,2},{1,3},{2,0},{3,1},{4,6},{5,7},{6,4},{7,5},{8,10},{9,11},{10,... | collective-permute-start | bytes 589832 | tf_op jit(solution)/shard_map/ppermute | solution.py:464
  160.0 7.0 %collective-permute-start.15 = (bf16[8,16,768]{2,1,0:T(8,128)(2,1)S(1)}, bf16[8,16,768]{2,1,0:T(8,128)(2,1)S(1)}, u32[]{:S(2)}, u32[]{:S(2)}) collective-permute-start(bf16[8,16,768]{2,1,0:T(8,128)(2,1)S(1)} %slice.173), channel_id=1, source_target_pairs={{0,2},{1,3},{2,0},{3,1},{4,6},{5,7},{6,4},{7,5},{8,10},{9,11},{10,... | collective-permute-start | bytes 589832 | tf_op jit(solution)/shard_map/ppermute | solution.py:464
  198.5 22.0 %collective-permute-start.20 = (bf16[8,48,768]{2,1,0:T(8,128)(2,1)}, bf16[8,48,768]{2,1,0:T(8,128)(2,1)S(1)}, u32[]{:S(2)}, u32[]{:S(2)}) collective-permute-start(bf16[8,48,768]{2,1,0:T(8,128)(2,1)} %get-tuple-element.60), channel_id=1, source_target_pairs={{0,1},{1,0},{2,3},{3,2},{4,5},{5,4},{6,7},{7,6},{8,9},{9,8},{10,11... | collective-permute-start | bytes 1769480 | tf_op jit(solution)/shard_map/ppermute | solution.py:464
  220.0 37.9 %collective-permute-start.24 = (bf16[8,48,1152]{2,1,0:T(8,128)(2,1)}, bf16[8,48,1152]{2,1,0:T(8,128)(2,1)S(1)}, u32[]{:S(2)}, u32[]{:S(2)}) collective-permute-start(bf16[8,48,1152]{2,1,0:T(8,128)(2,1)} %get-tuple-element.63), channel_id=1, source_target_pairs={{0,1},{1,0},{2,3},{3,2},{4,5},{5,4},{6,7},{7,6},{8,9},{9,8},{10,11... | collective-permute-start | bytes 2654216 | tf_op jit(solution)/shard_map/ppermute | solution.py:464
  220.7 36.6 %collective-permute-start.21 = (bf16[4,48,768]{2,1,0:T(8,128)(2,1)S(1)}, bf16[4,48,768]{2,1,0:T(8,128)(2,1)S(1)}, u32[]{:S(2)}, u32[]{:S(2)}) collective-permute-start(bf16[4,48,768]{2,1,0:T(8,128)(2,1)S(1)} %slice.181), channel_id=1, source_target_pairs={{0,4},{1,9},{2,6},{3,11},{4,0},{5,13},{6,2},{7,15},{8,12},{9,1},{1... | collective-permute-start | bytes 884744 | tf_op jit(solution)/shard_map/ppermute | solution.py:505
  253.2 39.1 %collective-permute-start.30 = (f32[12,768]{1,0:T(8,128)S(1)}, f32[12,768]{1,0:T(8,128)S(1)}, u32[]{:S(2)}, u32[]{:S(2)}) collective-permute-start(f32[12,768]{1,0:T(8,128)S(1)} %pad_maximum_fusion.10), channel_id=1, source_target_pairs={{0,1},{1,0},{2,3},{3,2},{4,5},{5,4},{6,7},{7,6},{8,9},{9,8},{10,11... | collective-permute-start | bytes 110600 | tf_op jit(solution)/shard_map/ppermute | solution.py:464
  256.8 9.1 %collective-permute-start.16 = (bf16[8,48,1152]{2,1,0:T(8,128)(2,1)}, bf16[8,48,1152]{2,1,0:T(8,128)(2,1)S(1)}, u32[]{:S(2)}, u32[]{:S(2)}) collective-permute-start(bf16[8,48,1152]{2,1,0:T(8,128)(2,1)} %get-tuple-element.57), channel_id=1, source_target_pairs={{0,1},{1,0},{2,3},{3,2},{4,5},{5,4},{6,7},{7,6},{8,9},{9,8},{10,11... | collective-permute-start | bytes 2654216 | tf_op jit(solution)/shard_map/ppermute | solution.py:464
  257.4 8.3 %collective-permute-start.22 = (bf16[2,48,768]{2,1,0:T(8,128)(2,1)S(1)}, bf16[2,48,768]{2,1,0:T(8,128)(2,1)S(1)}, u32[]{:S(2)}, u32[]{:S(2)}) collective-permute-start(bf16[2,48,768]{2,1,0:T(8,128)(2,1)S(1)} %slice.183), channel_id=1, source_target_pairs={{0,8},{1,17},{2,10},{3,19},{4,12},{5,21},{6,14},{7,23},{8,0},{9,25... | collective-permute-start | bytes 442376 | tf_op jit(solution)/shard_map/ppermute | solution.py:505
  258.1 13.5 %collective-permute-start.25 = (bf16[4,48,1152]{2,1,0:T(8,128)(2,1)S(1)}, bf16[4,48,1152]{2,1,0:T(8,128)(2,1)S(1)}, u32[]{:S(2)}, u32[]{:S(2)}) collective-permute-start(bf16[4,48,1152]{2,1,0:T(8,128)(2,1)S(1)} %slice.188), channel_id=1, source_target_pairs={{0,4},{1,9},{2,6},{3,11},{4,0},{5,13},{6,2},{7,15},{8,12},{9,1},{1... | collective-permute-start | bytes 1327112 | tf_op jit(solution)/shard_map/ppermute | solution.py:505
  265.8 5.7 %collective-permute-start.23 = (bf16[1,48,768]{2,1,0:T(8,128)(2,1)S(1)}, bf16[1,48,768]{2,1,0:T(8,128)(2,1)S(1)}, u32[]{:S(2)}, u32[]{:S(2)}) collective-permute-start(bf16[1,48,768]{2,1,0:T(8,128)(2,1)S(1)} %slice.185), channel_id=1, source_target_pairs={{0,16},{1,5},{2,18},{3,7},{4,20},{5,1},{6,22},{7,3},{8,24},{9,13},... | collective-permute-start | bytes 221192 | tf_op jit(solution)/shard_map/ppermute | solution.py:505
  266.1 8.5 %collective-permute-start.17 = (bf16[4,48,1152]{2,1,0:T(8,128)(2,1)S(1)}, bf16[4,48,1152]{2,1,0:T(8,128)(2,1)}, u32[]{:S(2)}, u32[]{:S(2)}) collective-permute-start(bf16[4,48,1152]{2,1,0:T(8,128)(2,1)S(1)} %slice.175), channel_id=1, source_target_pairs={{0,4},{1,9},{2,6},{3,11},{4,0},{5,13},{6,2},{7,15},{8,12},{9,1},{1... | collective-permute-start | bytes 1327112 | tf_op jit(solution)/shard_map/ppermute | solution.py:505
  271.8 6.8 %collective-permute-start.26 = (bf16[2,48,1152]{2,1,0:T(8,128)(2,1)S(1)}, bf16[2,48,1152]{2,1,0:T(8,128)(2,1)S(1)}, u32[]{:S(2)}, u32[]{:S(2)}) collective-permute-start(bf16[2,48,1152]{2,1,0:T(8,128)(2,1)S(1)} %slice.190), channel_id=1, source_target_pairs={{0,8},{1,17},{2,10},{3,19},{4,12},{5,21},{6,14},{7,23},{8,0},{9,25... | collective-permute-start | bytes 663560 | tf_op jit(solution)/shard_map/ppermute | solution.py:505
  275.7 7.2 %collective-permute-start.18 = (bf16[2,48,1152]{2,1,0:T(8,128)(2,1)S(1)}, bf16[2,48,1152]{2,1,0:T(8,128)(2,1)S(1)}, u32[]{:S(2)}, u32[]{:S(2)}) collective-permute-start(bf16[2,48,1152]{2,1,0:T(8,128)(2,1)S(1)} %slice.177), channel_id=1, source_target_pairs={{0,8},{1,17},{2,10},{3,19},{4,12},{5,21},{6,14},{7,23},{8,0},{9,25... | collective-permute-start | bytes 663560 | tf_op jit(solution)/shard_map/ppermute | solution.py:505
  278.7 10.8 %collective-permute-start.27 = (bf16[1,48,1152]{2,1,0:T(8,128)(2,1)S(1)}, bf16[1,48,1152]{2,1,0:T(8,128)(2,1)S(1)}, u32[]{:S(2)}, u32[]{:S(2)}) collective-permute-start(bf16[1,48,1152]{2,1,0:T(8,128)(2,1)S(1)} %slice.192), channel_id=1, source_target_pairs={{0,16},{1,5},{2,18},{3,7},{4,20},{5,1},{6,22},{7,3},{8,24},{9,13},... | collective-permute-start | bytes 331784 | tf_op jit(solution)/shard_map/ppermute | solution.py:505
  283.0 7.7 %collective-permute-start.19 = (bf16[1,48,1152]{2,1,0:T(8,128)(2,1)S(1)}, bf16[1,48,1152]{2,1,0:T(8,128)(2,1)S(1)}, u32[]{:S(2)}, u32[]{:S(2)}) collective-permute-start(bf16[1,48,1152]{2,1,0:T(8,128)(2,1)S(1)} %slice.179), channel_id=1, source_target_pairs={{0,16},{1,5},{2,18},{3,7},{4,20},{5,1},{6,22},{7,3},{8,24},{9,13},... | collective-permute-start | bytes 331784 | tf_op jit(solution)/shard_map/ppermute | solution.py:505
  291.1 17.9 %collective-permute-start.28 = (bf16[48,4,384]{2,1,0:T(4,128)(2,1)S(1)}, bf16[48,4,384]{2,1,0:T(4,128)(2,1)S(1)}, u32[]{:S(2)}, u32[]{:S(2)}) collective-permute-start(bf16[48,4,384]{2,1,0:T(4,128)(2,1)S(1)} %broadcast_select_fusion.1), channel_id=1, source_target_pairs={{0,2},{1,3},{2,0},{3,1},{4,6},{5,7},{6,4},{7,5},{8,10},{9,11},{10,... | collective-permute-start | bytes 442376 | tf_op jit(solution)/shard_map/ppermute | solution.py:464
  292.3 4.5 %collective-permute-start.31 = (f32[12,768]{1,0:T(8,128)S(1)}, f32[12,768]{1,0:T(8,128)S(1)}, u32[]{:S(2)}, u32[]{:S(2)}) collective-permute-start(f32[12,768]{1,0:T(8,128)S(1)} %fusion.4), channel_id=1, source_target_pairs={{0,2},{1,3},{2,0},{3,1},{4,6},{5,7},{6,4},{7,5},{8,10},{9,11},{10,... | collective-permute-start | bytes 110600 | tf_op jit(solution)/shard_map/ppermute | solution.py:464
  301.0 4.5 %collective-permute-start.33 = (f32[12,768]{1,0:T(8,128)S(1)}, f32[12,768]{1,0:T(8,128)S(1)}, u32[]{:S(2)}, u32[]{:S(2)}) collective-permute-start(f32[12,768]{1,0:T(8,128)S(1)} %add.126), channel_id=1, source_target_pairs={{0,8},{1,9},{2,10},{3,11},{4,12},{5,13},{6,14},{7,15},{8,0},{9,1},... | collective-permute-start | bytes 110600 | tf_op jit(solution)/shard_map/ppermute | solution.py:464
  305.5 16.4 %collective-permute-start.34 = (f32[12,768]{1,0:T(8,128)S(1)}, f32[12,768]{1,0:T(8,128)S(1)}, u32[]{:S(2)}, u32[]{:S(2)}) collective-permute-start(f32[12,768]{1,0:T(8,128)S(1)} %add.127), channel_id=1, source_target_pairs={{0,16},{1,17},{2,18},{3,19},{4,20},{5,21},{6,22},{7,23},{8,24},{9,... | collective-permute-start | bytes 110600 | tf_op jit(solution)/shard_map/ppermute | solution.py:464
  310.0 13.1 %collective-permute-start.29 = (f32[48,4,192]{2,0,1:T(8,128)S(1)}, f32[48,4,192]{2,0,1:T(8,128)S(1)}, u32[]{:S(2)}, u32[]{:S(2)}) collective-permute-start(f32[48,4,192]{2,0,1:T(8,128)S(1)} %bitcast.56), channel_id=1, source_target_pairs={{0,1},{1,0},{2,3},{3,2},{4,5},{5,4},{6,7},{7,6},{8,9},{9,8},{10,11... | collective-permute-start | bytes 442376 | tf_op jit(solution)/shard_map/ppermute | solution.py:464
  (10 other events, 46.2 us)

commit v2 on v1

--- a/solution.py
+++ b/solution.py
@@ -28,12 +28,16 @@
     return pltpu.CompilerParams(vmem_limit_bytes=VMEM_LIMIT)
 
 
-def whole(shape):
-    return pl.BlockSpec(shape, lambda i: (0,) * len(shape))
+def cost(flops, moved):
+    return pl.CostEstimate(flops=int(flops), bytes_accessed=int(moved), transcendentals=0)
+
+
+def whole(shape, column=0):
+    return pl.BlockSpec(shape, lambda *_: (0,) * (len(shape) - 1) + (column,))
 
 
 def per_image(shape, column=0):
-    return pl.BlockSpec((1,) + shape, lambda i: (i, 0, column))
+    return pl.BlockSpec((1,) + shape, lambda i, *_: (i, 0, column))
 
 
 def layer_stats(values):
@@ -52,32 +56,58 @@
     return lax.broadcasted_iota(jnp.int32, shape, len(shape) - 2)
 
 
-def norm_kernel(x_ref, norms_ref, out_ref):
-    unit, _ = layer_stats(x_ref[0].astype(F32))
-    out_ref[0] = (unit * norms_ref[0:1, :] + norms_ref[1:2, :]).astype(BF)
-
-
-def first_norm(x_img, norms):
-    images, rows, width = x_img.shape
+def shift_ids(rows):
+    first = pl.program_id(0) * SEQ
+    start = pl.multiple_of((first // 8) * 8, 8)
+    return start, first - start
+
+
+def pad_kernel(x_ref, g_ref, x_out, g_out, x_wide, g_wide):
+    count = x_ref.shape[0]
+    for ref, out, wide in ((x_ref, x_out, x_wide), (g_ref, g_out, g_wide)):
+
+        @pl.when(pl.program_id(0) == 0)
+        def _():
+            wide[0:count, :] = ref[...].astype(F32)
+            wide[count:, :] = jnp.zeros((wide.shape[0] - count, wide.shape[1]), F32)
+
+        start, offset = shift_ids(count)
+        window = wide[pl.ds(start, PAD), :].astype(BF)
+        shape = (PAD, PAD)
+        pick = jnp.logical_and(lane_ids(shape) == row_ids(shape) + offset, row_ids(shape) < SEQ)
+        out[0] = dot(pick.astype(BF), window).astype(BF)
+
+
+def window_rows(count):
+    images = count // SEQ
+    return max(((images - 1) * SEQ // 8) * 8 + PAD, -(-count // 8) * 8)
+
+
+def pad_images(tokens, cotangent):
+    count, width = tokens.shape
+    images = count // SEQ
+    shape = jax.ShapeDtypeStruct((images, PAD, width), BF)
     return pl.pallas_call(
-        norm_kernel,
+        pad_kernel,
         grid=(images,),
-        in_specs=[per_image((rows, width)), whole(norms.shape)],
-        out_specs=per_image((rows, width)),
-        out_shape=jax.ShapeDtypeStruct((images, rows, width), BF),
+        in_specs=[whole(tokens.shape), whole(cotangent.shape)],
+        out_specs=[per_image((PAD, width))] * 2,
+        out_shape=[shape, shape],
+        scratch_shapes=[pltpu.VMEM((window_rows(count), width), F32)] * 2,
         compiler_params=params(),
-        name="first_norm",
-    )(x_img, norms)
-
-
-def attend_kernel(pairs, n_ref, w_ref, qkv_ref, mixed_ref, probs_ref):
-    span = pairs * 128
-    rows = n_ref.shape[1]
-    proj = dot(n_ref[0], w_ref[...])
+        cost_estimate=cost(4 * images * PAD * PAD * width, 16 * count * width),
+        name="pad_images",
+    )(tokens, cotangent)
+
+
+def attend_image(normed, w_ref, qkv_ref, mixed_ref, probs_ref):
+    span = mixed_ref.shape[2]
+    rows = normed.shape[0]
+    proj = dot(normed, w_ref[...])
     low = lane_ids((rows, 128)) < HEAD_DIM
     key_ok = row_ids((rows, rows)) < SEQ
     zero = jnp.zeros((rows, 128), BF)
-    for p in range(pairs):
+    for p in range(span // 128):
         at = slice(p * 128, (p + 1) * 128)
         q = (proj[:, p * 128 : (p + 1) * 128] * HEAD_DIM ** (-0.5)).astype(BF)
         k = proj[:, span + p * 128 : span + (p + 1) * 128].astype(BF)
@@ -99,27 +129,154 @@
         mixed_ref[0, :, at] = jnp.concatenate(mixed_t, axis=0).T.astype(BF)
 
 
-def attend(normed, weights):
-    images, rows, width = normed.shape
-    span = weights.shape[1] // 3
+def assemble_rows(tables, own_ref, sib_ref, pieces):
+    core_ref, own_place, sib_place = tables
+    core = core_ref[0]
+    part = own_ref.shape[1]
+    for k in range(own_ref.shape[0]):
+        for place, ref, which in ((own_place, own_ref, core), (sib_place, sib_ref, 1 - core)):
+            row = pl.multiple_of(2 * part * k + part * which, 16)
+            for lane, out_ref, at in pieces:
+                out_ref[pl.ds(row, part), at] = ref[place[k], :, lane : lane + at.stop - at.start]
+
+
+def assemble_smalls(place, ref, lane, norms_ref, router_ref):
+    count = ref.shape[0]
+    tile = jnp.concatenate([ref[place[k], 0:16, lane : lane + 128] for k in range(count)], axis=0)
+    width = norms_ref.shape[1]
+    columns = width // count
+    norms = 0.0
+    for k in range(count):
+        shape = (128, width)
+        spot = jnp.logical_and(lane_ids(shape) == row_ids(shape) + columns * k, row_ids(shape) < columns)
+        norms = norms + dot(tile[16 * k : 16 * k + 16], spot.astype(BF))
+    norms_ref[...] = norms[0:8]
+    shape = (count, 16 * count)
+    for j in range(width // 128):
+        spot = lane_ids(shape) == row_ids(shape) * 16 + 4 + j
+        router_ref[:, j * 128 : (j + 1) * 128] = dot(spot.astype(BF), tile).astype(BF)
+
+
+def attend_first_kernel(stepwise, *refs):
+    if stepwise:
+        tables, refs = refs[:3], refs[3:]
+        x_ref, own_ref, sib_ref, n_ref, qkv_ref, mixed_ref, probs_ref, w_ref, norms_ref, router_ref = refs
+
+        @pl.when(pl.program_id(0) == 0)
+        def _():
+            assemble_rows(tables, own_ref, sib_ref, [(0, w_ref, slice(0, w_ref.shape[1]))])
+            assemble_smalls(tables[1], own_ref, w_ref.shape[1], norms_ref, router_ref)
+    else:
+        x_ref, w_ref, norms_ref, n_ref, qkv_ref, mixed_ref, probs_ref = refs
+    unit, _ = layer_stats(x_ref[0].astype(F32))
+    normed = (unit * norms_ref[0:1, :] + norms_ref[1:2, :]).astype(BF)
+    n_ref[0] = normed
+    attend_image(normed, w_ref, qkv_ref, mixed_ref, probs_ref)
+
+
+def attend_second_kernel(stepwise, *refs):
+    if stepwise:
+        tables, refs = refs[:3], refs[3:]
+        n_ref, own_ref, sib_ref, qkv_ref, mixed_ref, probs_ref, w_ref, out_w_ref = refs
+        span = mixed_ref.shape[2]
+
+        @pl.when(pl.program_id(0) == 0)
+        def _():
+            assemble_rows(
+                tables,
+                own_ref,
+                sib_ref,
+                [
+                    (0, w_ref, slice(0, 3 * span)),
+                    (3 * span, out_w_ref, slice(span, 2 * span)),
+                    (4 * span, out_w_ref, slice(0, span)),
+                ],
+            )
+    else:
+        n_ref, w_ref, qkv_ref, mixed_ref, probs_ref = refs
+    attend_image(n_ref[0], w_ref, qkv_ref, mixed_ref, probs_ref)
+
+
+def attend_specs(images, rows, span):
     heads = span // HEAD_DIM
-    return pl.pallas_call(
-        functools.partial(attend_kernel, span // 128),
-        grid=(images,),
-        in_specs=[per_image((rows, width)), whole(weights.shape)],
-        out_specs=[
+    return (
+        [
             per_image((rows, 3 * span)),
             per_image((rows, span)),
-            pl.BlockSpec((1, heads, rows, rows), lambda i: (i, 0, 0, 0)),
-        ],
-        out_shape=[
+            pl.BlockSpec((1, heads, rows, rows), lambda i, *_: (i, 0, 0, 0)),
+        ],
+        [
             jax.ShapeDtypeStruct((images, rows, 3 * span), BF),
             jax.ShapeDtypeStruct((images, rows, span), BF),
             jax.ShapeDtypeStruct((images, heads, rows, rows), BF),
         ],
+    )
+
+
+def call_kernel(kernel, name, images, tables, operands, in_specs, out_specs, out_shape, flops, scratch=()):
+    moved = sum(o.size * o.dtype.itemsize for o in operands) + sum(
+        o.size * o.dtype.itemsize for o in out_shape
+    )
+    return pl.pallas_call(
+        kernel,
+        grid_spec=pltpu.PrefetchScalarGridSpec(
+            num_scalar_prefetch=len(tables),
+            grid=(images,),
+            in_specs=in_specs,
+            out_specs=out_specs,
+            scratch_shapes=list(scratch),
+        ),
+        out_shape=out_shape,
         compiler_params=params(),
-        name="attend",
-    )(normed, weights)
+        cost_estimate=cost(flops, moved),
+        name=name,
+    )(*tables, *operands)
+
+
+def attend_flops(images, rows, width, span):
+    return 2 * images * rows * (3 * width * span + 2 * rows * span)
+
+
+def attend_first(x_img, tables, operands, span, experts):
+    images, rows, width = x_img.shape
+    specs, shapes = attend_specs(images, rows, span)
+    specs = [per_image((rows, width))] + specs
+    shapes = [jax.ShapeDtypeStruct((images, rows, width), BF)] + shapes
+    if tables:
+        extra = [((width, 3 * span), BF), ((8, width), F32), ((experts, width), BF)]
+        specs += [whole(shape) for shape, _ in extra]
+        shapes += [jax.ShapeDtypeStruct(*e) for e in extra]
+    return call_kernel(
+        functools.partial(attend_first_kernel, bool(tables)),
+        "attend_first",
+        images,
+        tables,
+        (x_img,) + operands,
+        [per_image((rows, width))] + [whole(o.shape) for o in operands],
+        specs,
+        shapes,
+        attend_flops(images, rows, width, span),
+    )
+
+
+def attend_second(normed, tables, operands, span):
+    images, rows, width = normed.shape
+    specs, shapes = attend_specs(images, rows, span)
+    if tables:
+        extra = [((width, 3 * span), BF), ((width, 2 * span), BF)]
+        specs += [whole(shape) for shape, _ in extra]
+        shapes += [jax.ShapeDtypeStruct(*e) for e in extra]
+    return call_kernel(
+        functools.partial(attend_second_kernel, bool(tables)),
+        "attend_second",
+        images,
+        tables,
+        (normed,) + operands,
+        [per_image((rows, width))] + [whole(o.shape) for o in operands],
+        specs,
+        shapes,
+        attend_flops(images, rows, width, span),
+    )
 
 
 def softmaxes(logits):
@@ -226,7 +383,9 @@
     return pre * cdf, cdf + pre * density
 
 
-def expert_kernel(own_ref, near_ref, w1_ref, w2_ref, keep_ref, send_ref, d1_ref, d2_ref):
+def expert_kernel(
+    own_ref, near_ref, w1_ref, w2_ref, keep_ref, send_ref, slots_ref, grads_ref, hidden_ref, pre_ref
+):
     count = own_ref.shape[0]
     blocks = jnp.concatenate([own_ref[...], near_ref[...]], axis=0)
     slots, grads = split_rows(blocks)
@@ -239,23 +398,49 @@
     joined = join_rows(returned, grad_slots)
     keep_ref[...] = joined[:count]
     send_ref[...] = joined[count:]
-    d1_ref[...] = dot(slots, grad_pre, FIRST)
-    d2_ref[...] = dot(hidden, grads, FIRST)
+    slots_ref[...] = slots
+    grads_ref[...] = grads
+    hidden_ref[...] = hidden
+    pre_ref[...] = grad_pre
 
 
 def run_expert(own, near, first_weight, second_weight):
     width, units = first_weight.shape
+    rows = (own.shape[0] + near.shape[0]) * SLOT_ROWS // 2
     return pl.pallas_call(
         expert_kernel,
         out_shape=[
             jax.ShapeDtypeStruct(own.shape, BF),
             jax.ShapeDtypeStruct(near.shape, BF),
+            jax.ShapeDtypeStruct((rows, width), BF),
+            jax.ShapeDtypeStruct((rows, width), BF),
+            jax.ShapeDtypeStruct((rows, units), BF),
+            jax.ShapeDtypeStruct((rows, units), BF),
+        ],
+        compiler_params=params(),
+        cost_estimate=cost(8 * rows * width * units, 4 * width * units + 16 * rows * width),
+        name="expert",
+    )(own, near, first_weight, second_weight)
+
+
+def expert_grad_kernel(slots_ref, grads_ref, hidden_ref, pre_ref, d1_ref, d2_ref):
+    d1_ref[...] = dot(slots_ref[...], pre_ref[...], FIRST)
+    d2_ref[...] = dot(hidden_ref[...], grads_ref[...], FIRST)
+
+
+def expert_grads(slots, grads, hidden, grad_pre):
+    rows, width = slots.shape
+    units = hidden.shape[1]
+    return pl.pallas_call(
+        expert_grad_kernel,
+        out_shape=[
             jax.ShapeDtypeStruct((width, units), F32),
             jax.ShapeDtypeStruct((units, width), F32),
         ],
         compiler_params=params(),
-        name="expert",
-    )(own, near, first_weight, second_weight)
+        cost_estimate=cost(4 * rows * width * units, 8 * width * units + 8 * rows * width),
+        name="expert_grads",
+    )(slots, grads, hidden, grad_pre)
 
 
 def moe_back_kernel(
@@ -269,7 +454,6 @@
     out_w_ref,
     m1_ref,
     m2_ref,
-    out_ref,
     grad_y_ref,
     grad_mixed_ref,
     out_grad_ref,
@@ -286,7 +470,6 @@
     unit, inv_std = layer_stats(y)
     gain = norms_ref[2:3, :]
     normed = (unit * gain + norms_ref[3:4, :]).astype(BF)
-    out_ref[0] = (y + dot(combine.astype(BF), returned, FIRST)).astype(BF)
     grad_combine = dot(returned, g_low, LAST)
     grad_dispatch = dot(grad_slots, normed, LAST)
     grad_logits = dispatch * (
@@ -338,30 +521,91 @@
         out_specs=[
             per_image((rows, width)),
             per_image((rows, width)),
-            per_image((rows, width)),
             whole((width, width)),
             whole((8 + experts, width)),
         ],
         out_shape=[
-            jax.ShapeDtypeStruct((images, rows, width), BF),
             jax.ShapeDtypeStruct((images, rows, width), F32),
             jax.ShapeDtypeStruct((images, rows, width), BF),
             jax.ShapeDtypeStruct((width, width), F32),
             jax.ShapeDtypeStruct((8 + experts, width), F32),
         ],
         compiler_params=params(),
+        cost_estimate=cost(4 * images * rows * width * width, 14 * images * rows * width),
         name="moe_back",
     )(y, g_img, logits, back, norms, router, out_w, mixed_one, mixed_two)
 
 
-def attend_back_kernel(pairs, n_ref, qkv_ref, probs_ref, mixed_ref, gm_ref, grads_ref, dw_ref):
+def join_images(wide, padded, exact):
+    start, offset = shift_ids(wide.shape[0])
+    shape = (PAD, PAD)
+    pick = jnp.logical_and(row_ids(shape) == lane_ids(shape) + offset, lane_ids(shape) < SEQ).astype(BF)
+    high = padded.astype(BF)
+    moved = dot(pick, high)
+    if exact:
+        rest = padded - high.astype(F32)
+        middle = rest.astype(BF)
+        moved = moved + dot(pick, middle) + dot(pick, (rest - middle.astype(F32)).astype(BF))
+
+    @pl.when(pl.program_id(0) == 0)
+    def _():
+        wide[...] = jnp.zeros_like(wide)
+
+    wide[pl.ds(start, PAD), :] += moved
+
+
+def output_kernel(y_ref, logits_ref, back_ref, out_ref, wide):
     image = pl.program_id(0)
-    span = pairs * 128
+    experts = logits_ref.shape[1]
+    returned = dot(pick_rows(experts, image, 0), back_ref[...]).astype(BF)
+    _, combine = softmaxes(logits_ref[0])
+    join_images(wide, y_ref[0] + dot(combine.astype(BF), returned, FIRST), False)
+
+    @pl.when(image == pl.num_programs(0) - 1)
+    def _():
+        out_ref[...] = wide[0 : out_ref.shape[0], :].astype(BF)
+
+
+def block_output(y, logits, back):
+    images, rows, width = y.shape
+    count = images * SEQ
+    return pl.pallas_call(
+        output_kernel,
+        grid=(images,),
+        in_specs=[per_image((rows, width)), per_image(logits.shape[1:]), whole(back.shape)],
+        out_specs=whole((count, width)),
+        out_shape=jax.ShapeDtypeStruct((count, width), BF),
+        scratch_shapes=[pltpu.VMEM((window_rows(count), width), F32)],
+        compiler_params=params(),
+        cost_estimate=cost(2 * images * rows * rows * width, 6 * images * rows * width),
+        name="block_output",
+    )(y, logits, back)
+
+
+def deal_rows(tables, full_ref, own_ref, sib_ref, lane):
+    core_ref, own_place, sib_place = tables
+    core = core_ref[0]
+    count, part, _ = own_ref.shape
+    span = full_ref.shape[1]
+    for k in range(count):
+        for place, ref, which in ((own_place, own_ref, core), (sib_place, sib_ref, 1 - core)):
+            row = pl.multiple_of(2 * part * k + part * which, 16)
+            ref[place[k], :, lane : lane + span] = full_ref[pl.ds(row, part), :].astype(BF)
+
+
+def attend_back_kernel(stepwise, *refs):
+    if stepwise:
+        tables, refs = refs[:3], refs[3:]
+        n_ref, qkv_ref, probs_ref, mixed_ref, gm_ref, og_ref, grads_ref, own_ref, sib_ref, dw_ref = refs
+    else:
+        n_ref, qkv_ref, probs_ref, mixed_ref, gm_ref, grads_ref, dw_ref = refs
+    image = pl.program_id(0)
+    span = mixed_ref.shape[2]
     rows = n_ref.shape[1]
     low = lane_ids((rows, 128)) < HEAD_DIM
     zero = jnp.zeros((rows, 128), BF)
     minus = jnp.full((rows, 128), -1.0, BF)
-    for p in range(pairs):
+    for p in range(span // 128):
         at = slice(p * 128, (p + 1) * 128)
         q = qkv_ref[0, :, at]
         k = qkv_ref[0, :, span + p * 128 : span + (p + 1) * 128]
@@ -389,39 +633,61 @@
 
     dw_ref[...] += dot(n_ref[0], grads_ref[0], FIRST)
 
-
-def attend_back(normed, qkv, probs, mixed, grad_mixed, piece):
+    if stepwise:
+
+        @pl.when(image == pl.num_programs(0) - 1)
+        def _():
+            deal_rows(tables, dw_ref, own_ref, sib_ref, 0)
+            deal_rows(tables, og_ref, own_ref, sib_ref, 3 * span)
+
+
+def attend_back(normed, qkv, probs, mixed, grad_mixed, out_grad_t, piece, tables, sizes):
     images, rows, width = normed.shape
     span = mixed.shape[2]
     heads = span // HEAD_DIM
-    return pl.pallas_call(
-        functools.partial(attend_back_kernel, span // 128),
-        grid=(images,),
-        in_specs=[
-            per_image((rows, width)),
-            per_image((rows, 3 * span)),
-            pl.BlockSpec((1, heads, rows, rows), lambda i: (i, 0, 0, 0)),
-            per_image((rows, span)),
-            per_image((rows, span), piece),
-        ],
-        out_specs=[per_image((rows, 3 * span)), whole((width, 3 * span))],
-        out_shape=[
-            jax.ShapeDtypeStruct((images, rows, 3 * span), BF),
-            jax.ShapeDtypeStruct((width, 3 * span), F32),
-        ],
-        compiler_params=params(),
-        name="attend_back",
-    )(normed, qkv, probs, mixed, grad_mixed)
-
-
-def input_back_kernel(x_ref, gy_ref, p1_ref, p2_ref, w1_ref, w2_ref, norms_ref, out_ref, small_ref):
+    operands = (normed, qkv, probs, mixed, grad_mixed)
+    in_specs = [
+        per_image((rows, width)),
+        per_image((rows, 3 * span)),
+        pl.BlockSpec((1, heads, rows, rows), lambda i, *_: (i, 0, 0, 0)),
+        per_image((rows, span)),
+        per_image((rows, span), piece),
+    ]
+    out_specs = [per_image((rows, 3 * span))]
+    out_shape = [jax.ShapeDtypeStruct((images, rows, 3 * span), BF)]
+    scratch = ()
+    if tables:
+        operands += (out_grad_t,)
+        in_specs.append(whole((width, span), piece))
+        block = (sizes[0], width // sizes[0] // 2, 4 * span)
+        out_specs += [whole(block)] * 2
+        out_shape += [jax.ShapeDtypeStruct(block, BF)] * 2
+        scratch = (pltpu.VMEM((width, 3 * span), F32),)
+    else:
+        out_specs.append(whole((width, 3 * span)))
+        out_shape.append(jax.ShapeDtypeStruct((width, 3 * span), F32))
+    return call_kernel(
+        functools.partial(attend_back_kernel, bool(tables)),
+        "attend_back",
+        images,
+        tables,
+        operands,
+        in_specs,
+        out_specs,
+        out_shape,
+        2 * images * rows * (3 * width * span + 4 * rows * span),
+        scratch,
+    )
+
+
+def input_back_kernel(x_ref, gy_ref, p1_ref, p2_ref, w1_ref, w2_ref, norms_ref, out_ref, small_ref, wide):
     image = pl.program_id(0)
     unit, inv_std = layer_stats(x_ref[0].astype(F32))
     grad_one = dot(p1_ref[0], w1_ref[...], LAST) + dot(p2_ref[0], w2_ref[...], LAST)
     scaled = grad_one * norms_ref[0:1, :]
     mean_one = jnp.mean(scaled, axis=-1, keepdims=True)
     mean_two = jnp.mean(scaled * unit, axis=-1, keepdims=True)
-    out_ref[0] = gy_ref[0] + inv_std * (scaled - mean_one - unit * mean_two)
+    join_images(wide, gy_ref[0] + inv_std * (scaled - mean_one - unit * mean_two), True)
 
     @pl.when(image == 0)
     def _():
@@ -430,9 +696,14 @@
     small_ref[0:1, :] += jnp.sum(grad_one * unit, axis=0, keepdims=True)
     small_ref[1:2, :] += jnp.sum(grad_one, axis=0, keepdims=True)
 
+    @pl.when(image == pl.num_programs(0) - 1)
+    def _():
+        out_ref[...] = wide[0 : out_ref.shape[0], :]
+
 
 def input_back(x_img, grad_y, grads_one, grads_two, weight_one, weight_two, norms):
     images, rows, width = x_img.shape
+    count = images * SEQ
     return pl.pallas_call(
         input_back_kernel,
         grid=(images,),
@@ -445,14 +716,49 @@
             whole(weight_two.shape),
             whole(norms.shape),
         ],
-        out_specs=[per_image((rows, width)), whole((8, width))],
+        out_specs=[whole((count, width)), whole((8, width))],
         out_shape=[
-            jax.ShapeDtypeStruct((images, rows, width), F32),
+            jax.ShapeDtypeStruct((count, width), F32),
             jax.ShapeDtypeStruct((8, width), F32),
         ],
+        scratch_shapes=[pltpu.VMEM((window_rows(count), width), F32)],
         compiler_params=params(),
+        cost_estimate=cost(6 * images * rows * width * width, 18 * images * rows * width),
         name="input_back",
     )(x_img, grad_y, grads_one, grads_two, weight_one, weight_two, norms)
+
+
+def merge_kernel(place, own_ref, core_ref, high_ref, small_ref, out_ref):
+    count, part, span = own_ref.shape
+    width = small_ref.shape[1]
+    columns = width // count
+    for k in range(count):
+        total = own_ref[k].astype(F32) + core_ref[k].astype(F32) + high_ref[k].astype(F32)
+        out_ref[k, :, 0:span] = total.astype(BF)
+    norms = small_ref[0:16, :].astype(BF)
+    routers = small_ref[16 : 16 + count, :].astype(BF)
+    for k in range(count):
+        shape = (width, 128)
+        spot = jnp.logical_and(row_ids(shape) == lane_ids(shape) + columns * k, lane_ids(shape) < columns)
+        rows = dot(norms, spot.astype(BF))
+        shape = (16, count)
+        for j in range(width // 128):
+            spot = jnp.logical_and(row_ids(shape) == 4 + j, lane_ids(shape) == k)
+            rows = rows + dot(spot.astype(BF), routers[:, j * 128 : (j + 1) * 128])
+        out_ref[place[k], 0:16, span:] = rows.astype(BF)
+        out_ref[place[k], 16:, span:] = jnp.zeros((part - 16, 128), BF)
+
+
+def merge(place, own, from_core, from_high, small):
+    count, part, span = own.shape
+    return pl.pallas_call(
+        merge_kernel,
+        in_specs=[pl.BlockSpec(memory_space=pltpu.SMEM)] + [pl.BlockSpec(memory_space=pltpu.VMEM)] * 4,
+        out_shape=jax.ShapeDtypeStruct((count, part, span + 128), BF),
+        compiler_params=params(),
+        cost_estimate=cost(own.size, 8 * own.size),
+        name="merge",
+    )(place, own, from_core, from_high, small)
 
 
 def swap(value, dp_size, tensor_size, dp_mask, tensor_mask):
@@ -490,14 +796,6 @@
     return jnp.where(core == 0, both[0], both[1]), jnp.where(core == 0, both[1], both[0])
 
 
-def gather_steps(block, dp_size, tensor_size):
-    held = block[None]
-    for step in range(dp_size.bit_length() - 1):
-        got = lax.ppermute(held, AXES, step_pairs(dp_size, tensor_size, step))
-        held = jnp.concatenate([held, got], axis=0)
-    return held
-
-
 def scatter_steps(blocks, dp_size, tensor_size):
     held = blocks
     for step in range(dp_size.bit_length() - 1)[::-1]:
@@ -507,83 +805,49 @@
     return held[0]
 
 
-def assemble_kernel(part, core_ref, own_place, sib_place, own_ref, sib_ref, out_ref):
-    core = core_ref[0]
-    for k in range(own_ref.shape[0]):
-        for place, ref, which in ((own_place, own_ref, core), (sib_place, sib_ref, 1 - core)):
-            row = pl.multiple_of(2 * part * k + part * which, 16)
-            out_ref[pl.ds(row, part), :] = ref[place[k], 0:part, :]
-
-
-def assemble(own, sib, part, core, own_place, sib_place):
-    return pl.pallas_call(
-        functools.partial(assemble_kernel, part),
-        in_specs=[pl.BlockSpec(memory_space=pltpu.SMEM)] * 3 + [pl.BlockSpec(memory_space=pltpu.VMEM)] * 2,
-        out_shape=jax.ShapeDtypeStruct((own.shape[0] * 2 * part, own.shape[2]), BF),
-        compiler_params=params(),
-        name="assemble",
-    )(core, own_place, sib_place, own, sib)
-
-
-def deal_kernel(part, core_ref, own_place, sib_place, full_ref, own_ref, sib_ref):
-    core = core_ref[0]
-    for k in range(own_ref.shape[0]):
-        for place, ref, which in ((own_place, own_ref, core), (sib_place, sib_ref, 1 - core)):
-            row = pl.multiple_of(2 * part * k + part * which, 16)
-            ref[place[k]] = full_ref[pl.ds(row, part), :].astype(BF)
-
-
-def deal(full, part, dp_size, core, own_place, sib_place):
-    shape = jax.ShapeDtypeStruct((dp_size, part, full.shape[1]), BF)
-    return pl.pallas_call(
-        functools.partial(deal_kernel, part),
-        in_specs=[pl.BlockSpec(memory_space=pltpu.SMEM)] * 3 + [pl.BlockSpec(memory_space=pltpu.VMEM)],
-        out_shape=[shape, shape],
-        compiler_params=params(),
-        name="deal",
-    )(core, own_place, sib_place, full)
-
-
-def gather_weights(qkv_weight, out_weight, router, norm_params, sizes, ids, tables):
-    dp_size, tensor_size = sizes
-    dp_index, _, core = ids
-    rows = qkv_weight.shape[1]
-    columns = qkv_weight.shape[2]
-    width = rows * dp_size
-    half = width // 2
+def pick(core, zero, one):
+    return jnp.where(core == 0, zero, one), jnp.where(core == 0, one, zero)
+
+
+def gather_weights(qkv_weight, out_weight, router, norm_params, sizes, ids, along):
+    core, high = ids
+    rows, columns = qkv_weight.shape[1:]
     part = rows // 2
+    small = jnp.concatenate([jnp.pad(norm_params, ((0, 0), (0, columns - rows))), router.T], axis=0)
+    small_high = swap(small, *sizes, 0, 2)
     turned = jnp.concatenate([qkv_weight, out_weight.T[None]], axis=0)
-    turned = turned.transpose(1, 0, 2).reshape(rows, 4 * columns)
-    small = jnp.concatenate(
-        [jnp.pad(norm_params, ((0, 0), (0, 4 * columns - rows))), jnp.pad(router.T, ((0, 0), (0, 3 * columns)))],
-        axis=0,
-    )
-    packed = jnp.concatenate([turned, jnp.pad(small, ((0, 14), (0, 0)))], axis=0)
-    spread = lax.all_gather(packed, "tensor", axis=0)
-    norm_cols = spread[:, rows, :rows]
-    router_row = spread[:, rows + 1, :columns].reshape(1, width)
-    by_kind = spread[:, :rows].reshape(tensor_size, rows, 4, columns)
-    by_kind = lax.dynamic_slice_in_dim(by_kind, core * part, part, axis=1)
-    by_kind = by_kind.transpose(1, 2, 0, 3).reshape(part, 4, width)
-    one = by_kind[:, :3, :half].reshape(part, 3 * half)
-    two = by_kind[:, :3, half:].reshape(part, 3 * half)
-    out_rows = by_kind[:, 3]
-    experts = dp_size * router.shape[1]
-    extra_rows = -(-(4 + experts) // 16) * 16
-    extra = jnp.zeros((extra_rows, 3 * half), BF)
-    extra = lax.dynamic_update_slice(extra, norm_cols, (0, dp_index * rows))
-    extra = lax.dynamic_update_slice(extra, router_row, (4 + dp_index, 0))
-    got_one = gather_steps(jnp.concatenate([one, extra], axis=0), dp_size, tensor_size)
-    sib_one = swap(got_one, dp_size, tensor_size, 0, 1)
-    smalls = jnp.sum(got_one[:, part:, :width].astype(F32), axis=0)
-    got_two = gather_steps(two, dp_size, tensor_size)
-    sib_two = swap(got_two, dp_size, tensor_size, 0, 1)
-    got_out = gather_steps(out_rows, dp_size, tensor_size)
-    sib_out = swap(got_out, dp_size, tensor_size, 0, 1)
-    weight_one = assemble(got_one, sib_one, part, *tables)
-    weight_two = assemble(got_two, sib_two, part, *tables)
-    out_w = assemble(got_out, sib_out, part, *tables)
-    return weight_one, weight_two, out_w, smalls[:4], smalls[4 : 4 + experts].astype(BF)
+    keep = lax.dynamic_slice_in_dim(turned, core * part, part, axis=1)
+    give = lax.dynamic_slice_in_dim(turned, (1 - core) * part, part, axis=1)
+    got = swap(give, *sizes, 0, 1)
+    first, second = pick(core, keep, got)
+    mine = jnp.concatenate([first, second], axis=2)
+    mine = mine.transpose(1, 0, 2).reshape(part, 8 * columns)
+    other = swap(mine, *sizes, 0, 2)
+    small_pair = jnp.stack([small, small_high])
+    small_near = swap(small_pair, *sizes, 0, 1)
+    first, second = pick(core, small_pair, small_near)
+    by_core = jnp.stack([first, second], axis=1)
+    first, second = pick(high, by_core[0], by_core[1])
+    smalls = jnp.stack([first, second]).reshape(4, 2, columns)
+    norm_rows = jnp.pad(smalls[:, 0, :rows], ((0, 0), (0, 128 - rows)))
+    tile = jnp.concatenate([norm_rows, smalls[:, 1].reshape(-1, 128)], axis=0)
+    tile = jnp.pad(tile, ((0, part - tile.shape[0]), (0, 0)))
+    block_one = jnp.concatenate([mine[:, : 6 * columns], tile], axis=1)
+    block_two = jnp.concatenate([other, mine[:, 6 * columns :]], axis=1)
+    held_one, held_two = block_one[None], block_two[None]
+    steps = sizes[0].bit_length() - 1
+    for step in range(steps):
+        got = lax.ppermute(held_one, AXES, step_pairs(*sizes, step))
+        if step == 0:
+            got, along = lax.optimization_barrier((got, pad_images(*along)))
+        held_one = jnp.concatenate([held_one, got], axis=0)
+    sib_one = swap(held_one, *sizes, 0, 1)
+    held_one, held_two = lax.optimization_barrier((held_one, held_two))
+    for step in range(steps):
+        got = lax.ppermute(held_two, AXES, step_pairs(*sizes, step))
+        held_two = jnp.concatenate([held_two, got], axis=0)
+    sib_two = swap(held_two, *sizes, 0, 1)
+    return (held_one, sib_one), (held_two, sib_two), along
 
 
 def gather_weights_plain(qkv_weight, out_weight, router, norm_params):
@@ -598,13 +862,6 @@
     one = qkv[:, :, :half].transpose(1, 0, 2).reshape(width, 3 * half)
     two = qkv[:, :, half:].transpose(1, 0, 2).reshape(width, 3 * half)
     return one, two, out_w.T, norms.astype(F32), router.T
-
-
-def scatter_weight(full, part, sizes, tables):
-    dp_size, tensor_size = sizes
-    own, sib = deal(full, part, dp_size, *tables)
-    got = swap(sib, dp_size, tensor_size, 0, 1)
-    return scatter_steps((own.astype(F32) + got.astype(F32)).astype(BF), dp_size, tensor_size)
 
 
 def sum_small(values, sizes):
@@ -620,13 +877,27 @@
     return values
 
 
-def pad_images(rows):
-    images = rows.shape[0] // SEQ
-    return jnp.pad(rows.reshape(images, SEQ, -1), ((0, 0), (0, PAD - SEQ), (0, 0)))
-
-
-def trim_images(padded):
-    return padded[:, :SEQ].reshape(-1, padded.shape[2])
+def scatter_weights(own_one, got_core, got_high, small, sizes, ids, place, rows, columns):
+    core, tensor_index = ids
+    part = rows // 2
+    blocks = merge(place, own_one, got_core, got_high, small)
+    mine = scatter_steps(blocks, *sizes)
+    span = mine.shape[1] - 128
+    tile = mine[:, span:]
+    norm_grad = lax.dynamic_slice(tile, (tensor_index, 0), (1, rows)).astype(F32)
+    router_grad = lax.dynamic_slice(
+        tile[4 : 4 + tensor_count(span, columns) * columns // 128].reshape(-1), (tensor_index * columns,), (columns,)
+    )
+    by_core = mine[:, :span].reshape(part, 4, 2, columns)
+    keep, give = pick(core, by_core[:, :, 0], by_core[:, :, 1])
+    got = swap(give, *sizes, 0, 1)
+    top, bottom = pick(core, keep, got)
+    both = jnp.concatenate([top, bottom], axis=0).astype(F32).transpose(1, 0, 2)
+    return both[:3], both[3].T, router_grad.astype(F32).reshape(columns, 1), norm_grad
+
+
+def tensor_count(span, columns):
+    return span // (2 * columns)
 
 
 def on_device(
@@ -641,84 +912,89 @@
     half = width // 2
     rows = qkv_weight.shape[1]
     columns = qkv_weight.shape[2]
-    part = rows // 2
-    stepwise = rows % 32 == 0
-    x_img = pad_images(tokens)
-    g_img = pad_images(cotangent)
+    experts = dp_size * router.shape[1]
+    stepwise = rows % 32 == 0 and tensor_size == 4
+    tables = ()
     if stepwise:
         tables = (core.reshape(1).astype(jnp.int32),) + places(dp_size, dp_index, core)
-        weight_one, weight_two, out_w, norms, router_t = gather_weights(
-            qkv_weight, out_weight, router, norm_params, sizes, (dp_index, tensor_index, core), tables
+        pair_one, pair_two, (x_img, g_img) = gather_weights(
+            qkv_weight, out_weight, router, norm_params, sizes, (core, high), (tokens, cotangent)
         )
+        normed, qkv_one, mixed_one, probs_one, weight_one, norms, router_t = attend_first(
+            x_img, tables, pair_one, half, experts
+        )
+        qkv_two, mixed_two, probs_two, weight_two, out_w = attend_second(normed, tables, pair_two, half)
     else:
+        x_img, g_img = pad_images(tokens, cotangent)
         weight_one, weight_two, out_w, norms, router_t = gather_weights_plain(
             qkv_weight, out_weight, router, norm_params
         )
-    experts = router_t.shape[0]
-    normed = first_norm(x_img, norms)
-    qkv_one, mixed_one, probs_one = attend(normed, weight_one)
-    qkv_two, mixed_two, probs_two = attend(normed, weight_two)
+        normed, qkv_one, mixed_one, probs_one = attend_first(x_img, (), (weight_one, norms), half, experts)
+        qkv_two, mixed_two, probs_two = attend_second(normed, (), (weight_two,), half)
     y, logits, outgoing = route(x_img, mixed_one, mixed_two, out_w, norms, router_t, g_img)
 
     outgoing = outgoing.reshape(experts, SLOT_ROWS, width)
     arrived = lax.all_to_all(outgoing, "dp", split_axis=0, concat_axis=0, tiled=True)
-    across = swap(arrived, dp_size, tensor_size, 0, 2)
+    across = swap(arrived, *sizes, 0, 2)
     pair = jnp.concatenate([arrived, across], axis=0)
-    near = swap(pair, dp_size, tensor_size, 0, 1)
-    keep, away, first_grad, second_grad = run_expert(pair, near, expert_in[0], expert_out[0])
-    got = swap(away, dp_size, tensor_size, 0, 1)
+    near = swap(pair, *sizes, 0, 1)
+    keep, away, *kept = run_expert(pair, near, expert_in[0], expert_out[0])
+    first_grad, second_grad = expert_grads(*kept)
+    got = swap(away, *sizes, 0, 1)
     summed = (keep.astype(F32) + got.astype(F32)).astype(BF)
-    got = swap(summed[dp_size:], dp_size, tensor_size, 0, 2)
+    got = swap(summed[dp_size:], *sizes, 0, 2)
     summed = (summed[:dp_size].astype(F32) + got.astype(F32)).astype(BF)
     back = lax.all_to_all(summed, "dp", split_axis=0, concat_axis=0, tiled=True)
     back = back.reshape(experts * SLOT_ROWS, width)
 
-    out_img, grad_y, grad_mixed, out_grad_t, small_two = moe_back(
+    grad_y, grad_mixed, out_grad_t, small_two = moe_back(
         y, g_img, logits, back, norms, router_t, out_w, mixed_one, mixed_two
     )
-    grads_one, dw_one = attend_back(normed, qkv_one, probs_one, mixed_one, grad_mixed, 0)
-    grads_two, dw_two = attend_back(normed, qkv_two, probs_two, mixed_two, grad_mixed, 1)
-    in_img, small_one = input_back(
+    output = block_output(y, logits, back)
+    grads_two, *dealt = attend_back(
+        normed, qkv_two, probs_two, mixed_two, grad_mixed, out_grad_t, 1, tables, sizes
+    )
+    if stepwise:
+        own, sib = dealt
+        got = swap(sib, *sizes, 0, 1)
+        paired = (own.astype(F32) + got.astype(F32)).astype(BF)
+        paired, grad_mixed = lax.optimization_barrier((paired, grad_mixed))
+        got_high = swap(paired, *sizes, 0, 2)
+    grads_one, *dealt_one = attend_back(
+        normed, qkv_one, probs_one, mixed_one, grad_mixed, out_grad_t, 0, tables, sizes
+    )
+    if stepwise:
+        own, sib = dealt_one
+        got_core = swap(sib, *sizes, 0, 1)
+    input_grad, small_one = input_back(
         x_img, grad_y, grads_one, grads_two, weight_one, weight_two, norms
     )
-    small = sum_small(
-        jnp.concatenate([small_one[0:2], small_two[0:2], small_two[8:]], axis=0), sizes
-    )
-    norm_grad = lax.dynamic_slice(small, (tensor_index, dp_index * rows), (1, rows))
-    router_grad = lax.dynamic_slice(
-        small, (4 + dp_index, tensor_index * columns), (1, columns)
-    ).reshape(columns, 1)
-
+    small = jnp.concatenate([small_one[0:2], small_two[0:2], small_two[8:]], axis=0)
     if stepwise:
-        one = scatter_weight(dw_one, part, sizes, tables).reshape(part, 3, half)
-        two = scatter_weight(dw_two, part, sizes, tables).reshape(part, 3, half)
-        out_t = scatter_weight(out_grad_t, part, sizes, tables).reshape(part, 2, half)
-        stacked = jnp.stack(
-            [jnp.concatenate([one, out_t[:, :1]], axis=1), jnp.concatenate([two, out_t[:, 1:]], axis=1)]
+        small = small + swap(small, *sizes, 0, 1)
+        small = small + swap(small, *sizes, 0, 2)
+        small = jnp.concatenate(
+            [small[:4], jnp.zeros((12, width), F32), small[4:], jnp.zeros((-experts % 16, width), F32)], axis=0
         )
-        mine = jnp.where(high == 0, stacked[0], stacked[1])
-        other = jnp.where(high == 0, stacked[1], stacked[0])
-        got = swap(other, dp_size, tensor_size, 0, 2)
-        total = (mine.astype(F32) + got.astype(F32)).reshape(part, 4, 2, columns)
-        keep = jnp.where(core == 0, total[:, :, 0], total[:, :, 1])
-        give = jnp.where(core == 0, total[:, :, 1], total[:, :, 0])
-        got = swap(give, dp_size, tensor_size, 0, 1)
-        top = jnp.where(core == 0, keep, got)
-        bottom = jnp.where(core == 0, got, keep)
-        both = jnp.concatenate([top, bottom], axis=0).transpose(1, 0, 2)
-        qkv_grad = both[:3]
-        out_grad = both[3].T
+        qkv_grad, out_grad, router_grad, norm_grad = scatter_weights(
+            own, got_core, got_high, small, sizes, (core, tensor_index), tables[1], rows, columns
+        )
     else:
+        small = sum_small(small, sizes)
+        norm_grad = lax.dynamic_slice(small, (tensor_index, dp_index * rows), (1, rows))
+        router_grad = lax.dynamic_slice(
+            small, (4 + dp_index, tensor_index * columns), (1, columns)
+        ).reshape(columns, 1)
         full = jnp.concatenate(
-            [dw_one.reshape(width, 3, half), dw_two.reshape(width, 3, half)], axis=2
+            [dealt_one[0].reshape(width, 3, half), dealt[0].reshape(width, 3, half)], axis=2
         ).transpose(1, 0, 2)
         qkv_grad = lax.psum_scatter(full, "dp", scatter_dimension=1, tiled=True)
         qkv_grad = lax.psum_scatter(qkv_grad, "tensor", scatter_dimension=2, tiled=True)
         out_grad = lax.psum_scatter(out_grad_t.T, "dp", scatter_dimension=1, tiled=True)
         out_grad = lax.psum_scatter(out_grad, "tensor", scatter_dimension=0, tiled=True)
     return (
-        trim_images(out_img),
-        trim_images(in_img),
+        output,
+        input_grad,
         qkv_grad,
         out_grad,
         router_grad,

time: 326 us -> 303 us (0.929)
  local copies, waits for them, and re-layouts: 31.5 us -> 9.01 us
  Pallas kernels: 135 us -> 147 us
  blocking collectives: 33.9 us -> 23.4 us
  starting transfers between devices: 32.9 us -> 23.4 us
  waiting for transfers between devices: 82.7 us -> 88.8 us
    reshape x10 -> x4, local copies, waits for them, and re-layouts: 12.2 us -> 0.25 us  [the longest x1 0.21 us: scatter_weights(): by_core = mine[:, :span].reshape(part, 4, 2, columns)]
    all_gather x1 -> x0, blocking collectives: 9.54 us -> none  [gather_weights(): spread = lax.all_gather(packed, 'tensor', axis=0)]
    slice x12 -> x10, local copies, waits for them, and re-layouts: 7.93 us -> 0.36 us  [the longest x1 0.28 us: scatter_weights(): keep, give = pick(core, by_core[:, :, 0], by_core[:, :, 1])]
    pallas_call x1, Pallas kernels: 12.7 us -> 20.1 us  [input_back(): pl.pallas_call(input_back_kernel, grid=(images,), in_specs=[per_image((ro...]
    ppermute x9 -> x3, starting transfers between devices: 8.78 us -> 1.36 us  [scatter_steps(): lax.ppermute(held[half:], AXES, step_pairs(dp_size, tensor_size, step))]
    pallas_call x11 -> x8, Pallas kernels: 85.7 us -> 92.1 us  [the longest x4 69.7 us: call_kernel(): pl.pallas_call(kernel, grid_spec=pltpu.PrefetchScalarGridSpec(num_scalar_...]
    ppermute x17 -> x16, waiting for transfers between devices: 24.4 us -> 29.9 us  [swap(): return lax.ppermute(value, AXES, pairs)]
    ppermute x9 -> x6, waiting for transfers between devices: 35 us -> 39.3 us  [the longest x3 30.9 us: gather_weights(): got = lax.ppermute(held_two, AXES, step_pairs(*sizes, step))]
  transfers between devices with their start and end apart: 35 -> 25, of which waited for: 20 -> 18; matrix products, arithmetic and copies ran while one was open for 10% -> 2% of each run, Pallas kernels for 24% -> 18%
where the time goes in v2:
time: 303 us; the launch traced here: 302 us
  Pallas kernels  147 us (49%)
  waiting for transfers between devices  88.8 us (29%)
  starting transfers between devices  23.4 us (8%)
  blocking collectives  23.4 us (8%)
  other arithmetic  9.48 us (3%)
  local copies, waits for them, and re-layouts  9.01 us (3%)
    pallas_call x4, Pallas kernels, call_kernel(): pl.pallas_call(kernel, grid_spec=pltpu.PrefetchScalarGridSpec(num_scalar_...  69.7 us
    ppermute x3, waiting for transfers between devices, gather_weights(): got = lax.ppermute(held_two, AXES, step_pairs(*sizes, step))  30.9 us
    ppermute x16, waiting for transfers between devices, swap(): return lax.ppermute(value, AXES, pairs)  29.9 us
    pallas_call x1, Pallas kernels, input_back(): pl.pallas_call(input_back_kernel, grid=(images,), in_specs=[per_image((ro...  20.1 us
    ppermute x3, waiting for transfers between devices, scatter_steps(): lax.ppermute(held[half:], AXES, step_pairs(dp_size, tensor_size, step))  19.6 us
    pallas_call x1, Pallas kernels, moe_back(): pl.pallas_call(functools.partial(moe_back_kernel, half), grid=(images,),...  17.1 us
    pallas_call x1, Pallas kernels, route(): pl.pallas_call(functools.partial(route_kernel, half), grid=(images,), in_...  13.2 us
    ppermute x16, starting transfers between devices, swap(): return lax.ppermute(value, AXES, pairs)  11.9 us
  transfers between devices with their start and end apart: 25, of which 18 were waited for; matrix products, arithmetic and copies ran while one was open for 2% of the time, Pallas kernels for 18%

profile of v2, /device:TPU:0, one launch (start us, length us, event | category | flops | bytes accessed | tf_op | source)
XLA Modules:
  0.0 302.2 jit_solution(16805431588127424827)
XLA Ops:
  1.3 3.0 %collective-permute-start.1 = (bf16[2,192]{1,0:T(2,128)(2,1)S(1)}, bf16[2,192]{1,0:T(2,128)(2,1)S(1)}, u32[]{:S(2)}, u32[]{:S(2)}) collective-permute-start(bf16[2,192]{1,0:T(2,128)(2,1)S(1)} %fusion.11), channel_id=1, source_target_pairs={{0,2},{1,3},{2,0},{3,1},{4,6},{5,7},{6,4},{7,5},{8,10},{9,11},{10,... | collective-permute-start | bytes 2312 | tf_op jit(solution)/shard_map/ppermute | solution.py:770
  9.7 3.1 %collective-permute-start.3 = (bf16[1,48,1280]{2,1,0:T(8,128)(2,1)S(1)}, bf16[1,48,1280]{2,1,0:T(8,128)(2,1)S(1)}, u32[]{:S(2)}, u32[]{:S(2)}) collective-permute-start(bf16[1,48,1280]{2,1,0:T(8,128)(2,1)S(1)} %fusion.3), channel_id=1, source_target_pairs={{0,16},{1,5},{2,18},{3,7},{4,20},{5,1},{6,22},{7,3},{8,24},{9,13},... | collective-permute-start | bytes 368648 | tf_op jit(solution)/shard_map/ppermute | solution.py:840
  12.8 6.9 %pad_images.1 = (bf16[6,208,768]{2,1,0:T(8,128)(2,1)}, bf16[6,208,768]{2,1,0:T(8,128)(2,1)}) custom-call(bf16[1182,768]{1,0:T(8,128)(2,1)} %x_ref.1, bf16[1182,768]{1,0:T(8,128)(2,1)} %g_ref.1), custom_call_target="tpu_custom_call" | custom-call | flops 797442048 | bytes 14524416 | tf_op jit(solution)/shard_map/pad_images/pallas_call | solution.py:90
  21.3 6.2 %collective-permute-done.4 = bf16[2,48,1280]{2,1,0:T(8,128)(2,1)S(1)} collective-permute-done((bf16[2,48,1280]{2,1,0:T(8,128)(2,1)S(1)}, bf16[2,48,1280]{2,1,0:T(8,128)(2,1)S(1)}, u32[]{:S(2)}, u32[]{:S(2)}) %collective-permute-start.4) | collective-permute-done | bytes 245792 | tf_op jit(solution)/shard_map/ppermute | solution.py:840
  30.5 3.6 %collective-permute-done.6 = bf16[48,1536]{1,0:T(8,128)(2,1)S(1)} collective-permute-done((bf16[48,1536]{1,0:T(8,128)(2,1)S(1)}, bf16[48,1536]{1,0:T(8,128)(2,1)S(1)}, u32[]{:S(2)}, u32[]{:S(2)}) %collective-permute-start.6) | collective-permute-done | bytes 147488 | tf_op jit(solution)/shard_map/ppermute | solution.py:770
  34.1 2.3 collective-permute-done.5
  37.4 12.3 %collective-permute-done.8 = bf16[1,48,1920]{2,1,0:T(8,128)(2,1)S(1)} collective-permute-done((bf16[1,48,1920]{2,1,0:T(8,128)(2,1)S(1)}, bf16[1,48,1920]{2,1,0:T(8,128)(2,1)S(1)}, u32[]{:S(2)}, u32[]{:S(2)}) %collective-permute-start.8) | collective-permute-done | bytes 184352 | tf_op jit(solution)/shard_map/ppermute | solution.py:847
  49.8 9.2 %collective-permute-done.9 = bf16[2,48,1920]{2,1,0:T(8,128)(2,1)S(1)} collective-permute-done((bf16[2,48,1920]{2,1,0:T(8,128)(2,1)S(1)}, bf16[2,48,1920]{2,1,0:T(8,128)(2,1)S(1)}, u32[]{:S(2)}, u32[]{:S(2)}) %collective-permute-start.9) | collective-permute-done | bytes 368672 | tf_op jit(solution)/shard_map/ppermute | solution.py:847
  59.1 3.1 %collective-permute-start.10 = (bf16[4,48,1920]{2,1,0:T(8,128)(2,1)S(1)}, bf16[4,48,1920]{2,1,0:T(8,128)(2,1)S(1)}, u32[]{:S(2)}, u32[]{:S(2)}) collective-permute-start(bf16[4,48,1920]{2,1,0:T(8,128)(2,1)S(1)} %pad_maximum_fusion.1), channel_id=1, source_target_pairs={{0,4},{1,9},{2,6},{3,11},{4,0},{5,13},{6,2},{7,15},{8,12},{9,1},{1... | collective-permute-start | bytes 2211848 | tf_op jit(solution)/shard_map/ppermute | solution.py:847
  62.3 9.4 %collective-permute-done.10 = bf16[4,48,1920]{2,1,0:T(8,128)(2,1)S(1)} collective-permute-done((bf16[4,48,1920]{2,1,0:T(8,128)(2,1)S(1)}, bf16[4,48,1920]{2,1,0:T(8,128)(2,1)S(1)}, u32[]{:S(2)}, u32[]{:S(2)}) %collective-permute-start.10) | collective-permute-done | bytes 737312 | tf_op jit(solution)/shard_map/ppermute | solution.py:847
  72.9 3.6 %collective-permute-done.7.refs_5_ = bf16[8,48,1280]{2,1,0:T(8,128)(2,1)S(1)} collective-permute-done((bf16[8,48,1280]{2,1,0:T(8,128)(2,1)S(1)}, bf16[8,48,1280]{2,1,0:T(8,128)(2,1)S(1)}, u32[]{:S(2)}, u32[]{:S(2)}) %collective-permute-start.7) | collective-permute-done | bytes 983072 | tf_op jit(solution)/shard_map/ppermute | solution.py:770
  77.4 16.0 %attend_first.1 = (bf16[6,208,768]{2,1,0:T(8,128)(2,1)}, bf16[6,208,1152]{2,1,0:T(8,128)(2,1)}, bf16[6,208,384]{2,1,0:T(8,128)(2,1)}, bf16[6,6,208,208]{3,2,1,0:...) custom-call(s32[1]{0:T(128)} %bitcast.10.refs_0_, ...), custom_call_target="tpu_custom_call" | custom-call | flops 2607022080 | bytes 14555136 | tf_op jit(solution)/shard_map/attend_first/pallas_call | solution.py:220
  93.5 14.6 %attend_second.1 = (bf16[6,208,1152]{2,1,0:T(8,128)(2,1)}, bf16[6,208,384]{2,1,0:T(8,128)(2,1)}, bf16[6,6,208,208]{3,2,1,0:T(8,128)(2,1)}, bf16[768,1152]{1,0:T(8,128)(2,1)}, bf16[768,768]{1,0:T(8,128)(2,1)}) custom-call(s32[1]{0:T(128)} %bitcast.10.refs_0_, s32[8]{0:T(128)} %get-tuple-element.115.refs_1_.place, s32[8]{0:T(128)} %get-tuple-element.114.refs_2_, ...), custom_call_target="tpu_custom_call" | custom-call | flops 2607022080 | bytes 14764032 | tf_op jit(solution)/shard_map/attend_second/pallas_call | solution.py:220
  108.0 13.2 %route.1 = (f32[6,208,768]{2,1,0:T(8,128)}, f32[6,8,208]{2,1,0:T(8,128)}, bf16[128,768]{1,0:T(8,128)(2,1)}) custom-call(bf16[6,208,768]{2,1,0:T(8,128)(2,1)} %get-tuple-element.54.refs_3_.x_ref, bf16[6,208,384]{2,1,0:T(8,128)(2,1)} %get-tuple-element.57.m1_ref.refs_6_, bf16[6,208,384]{2,1,0:T(8,128)(2,1)} %get-tuple-element.60.m2_ref.refs_6_, ...), custom_call_target="tpu_custom_call" | custom-call | tf_op jit(solution)/shard_map/route/pallas_call | solution.py:339
  121.3 11.8 %all_to_all.10 = bf16[8,16,768]{2,1,0:T(8,128)(2,1)S(1)} all-to-all(bf16[8,16,768]{2,1,0:T(8,128)(2,1)} %bitcast.53), channel_id=1, replica_groups=mesh['dp'=8,'tensor'=4] {'dp'}, dimensions={0} | all-to-all | bytes 393216 | tf_op jit(solution)/shard_map/all_to_all | solution.py:937
  134.8 4.0 %collective-permute-done.12 = bf16[8,16,768]{2,1,0:T(8,128)(2,1)S(1)} collective-permute-done((bf16[8,16,768]{2,1,0:T(8,128)(2,1)S(1)}, bf16[8,16,768]{2,1,0:T(8,128)(2,1)S(1)}, u32[]{:S(2)}, u32[]{:S(2)}) %collective-permute-start.12) | collective-permute-done | bytes 196640 | tf_op jit(solution)/shard_map/ppermute | solution.py:770
  141.4 4.4 %expert.1 = (bf16[16,16,768]{2,1,0:T(8,128)(2,1)}, bf16[16,16,768]{2,1,0:T(8,128)(2,1)}, bf16[256,768]{1,0:T(8,128)(2,1)}, bf16[256,768]{1,0:T(8,128)(2,1)}, bf1...) custom-call(bf16[16,16,768]{2,1,0:T(8,128)(2,1)} %copy-done.4, bf16[16,16,768]{2,1,0:T(8,128)(2,1)} %copy-done.8, ...), custom_call_target="tpu_custom_call" | custom-call | flops 1207959552 | bytes 5505024 | tf_op jit(solution)/shard_map/expert/pallas_call | solution.py:410
  145.9 1.8 collective-permute-done.14
  148.8 1.7 collective-permute-start.15
  150.6 5.3 %collective-permute-done.15 = bf16[8,16,768]{2,1,0:T(8,128)(2,1)S(1)} collective-permute-done((bf16[8,16,768]{2,1,0:T(8,128)(2,1)S(1)}, bf16[8,16,768]{2,1,0:T(8,128)(2,1)S(1)}, u32[]{:S(2)}, u32[]{:S(2)}) %collective-permute-start.15) | collective-permute-done | bytes 196640 | tf_op jit(solution)/shard_map/ppermute | solution.py:770
  155.9 11.6 %all_to_all.11 = bf16[8,16,768]{2,1,0:T(8,128)(2,1)} all-to-all(bf16[8,16,768]{2,1,0:T(8,128)(2,1)S(1)} %add_convert_fusion.4), channel_id=1, replica_groups=mesh['dp'=8,'tensor'=4] {'dp'}, dimensions={0} | all-to-all | bytes 393216 | tf_op jit(solution)/shard_map/all_to_all | solution.py:947
  167.5 17.1 %moe_back.1 = (f32[6,208,768]{2,1,0:T(8,128)}, bf16[6,208,768]{2,1,0:T(8,128)(2,1)}, f32[768,768]{1,0:T(8,128)}, f32[16,768]{1,0:T(8,128)}) custom-call(f32[6,208,768]{2,1,0:T(8,128)} %get-tuple-element.65.y_ref, bf16[6,208,768]{2,1,0:T(8,128)(2,1)} %get-tuple-element.64.g_ref, f32[6,8,208]{2,1,0:T(8,128)} %get-tuple-element.66.logits_ref, ...), custom_call_target="tpu_custom_call" | custom-call | flops 2944401408 | bytes 13418496 | tf_op jit(solution)/shard_map/moe_back/pallas_call | solution.py:507
  184.5 19.4 %attend_back.2 = (bf16[6,208,1152]{2,1,0:T(8,128)(2,1)}, bf16[8,48,1536]{2,1,0:T(8,128)(2,1)}, bf16[8,48,1536]{2,1,0:T(8,128)(2,1)}) custom-call(s32[1]{0:T(128)} %bitcast.10.refs_0_, s32[8]{0:T(128)} %get-tuple-element.115.refs_1_.place, s32[8]{0:T(128)} %get-tuple-element.114.refs_2_, bf16[6,208,768]{2,1,0:T(8,128)(2,1)} %get-tuple-element.58.refs_3_, ...), custom_call_target="tpu_custom_call" | custom-call | flops 3005743104 | bytes 18376704 | tf_op jit(solution)/shard_map/attend_back/pallas_call | solution.py:220
  204.0 3.0 %collective-permute-done.16 = bf16[8,48,1536]{2,1,0:T(8,128)(2,1)S(1)} collective-permute-done((bf16[8,48,1536]{2,1,0:T(8,128)(2,1)}, bf16[8,48,1536]{2,1,0:T(8,128)(2,1)S(1)}, u32[]{:S(2)}, u32[]{:S(2)}) %collective-permute-start.16) | collective-permute-done | bytes 1179680 | tf_op jit(solution)/shard_map/ppermute | solution.py:770
  208.6 19.6 %attend_back.3 = (bf16[6,208,1152]{2,1,0:T(8,128)(2,1)}, bf16[8,48,1536]{2,1,0:T(8,128)(2,1)}, bf16[8,48,1536]{2,1,0:T(8,128)(2,1)}) custom-call(s32[1]{0:T(128)} %bitcast.10.refs_0_, s32[8]{0:T(128)} %get-tuple-element.115.refs_1_.place, s32[8]{0:T(128)} %get-tuple-element.114.refs_2_, bf16[6,208,768]{2,1,0:T(8,128)(2,1)} %get-tuple-element.58.refs_3_, ...), custom_call_target="tpu_custom_call" | custom-call | flops 3005743104 | bytes 18376704 | tf_op jit(solution)/shard_map/attend_back/pallas_call | solution.py:220
  230.1 20.1 %input_back.1 = (f32[1182,768]{1,0:T(8,128)}, f32[8,768]{1,0:T(8,128)}) custom-call(bf16[6,208,768]{2,1,0:T(8,128)(2,1)} %get-tuple-element.54.refs_3_.x_ref, f32[6,208,768]{2,1,0:T(8,128)} %get-tuple-element.70.gy_ref, bf16[6,208,1152]{2,1,0:T(8,128)(2,1)} %get-tuple-element.80.p1_ref, bf16[6,208,1152]{2,1,0:T(8,128)(2,1)} %get-tuple-element.81.p2_ref, ...), custom_call_target="tpu_custom_call" | custom-call | flops 4416602112 | bytes 17252352 | tf_op jit(solution)/shard_map/input_back/pallas_call | solution.py:707
  252.9 4.8 %collective-permute-done.20 = f32[12,768]{1,0:T(8,128)S(1)} collective-permute-done((f32[12,768]{1,0:T(8,128)S(1)}, f32[12,768]{1,0:T(8,128)S(1)}, u32[]{:S(2)}, u32[]{:S(2)}) %collective-permute-start.20) | collective-permute-done | bytes 36896 | tf_op jit(solution)/shard_map/ppermute | solution.py:770
  259.8 3.8 %merge.1 = bf16[8,48,1664]{2,1,0:T(8,128)(2,1)} custom-call(s32[8]{0:T(128)} %get-tuple-element.115.refs_1_.place, bf16[8,48,1536]{2,1,0:T(8,128)(2,1)} %get-tuple-element.85.own_ref, bf16[8,48,1536]{2,1,0:T(8,128)(2,1)} %copy-done.1, bf16[8,48,1536]{2,1,0:T(8,128)(2,1)} %copy-done.2, f32[32,768]{1,0:T(8,128)} %maximum_maximum_fusion.small_ref), custom_call_target="tpu_custom_call" | custom-call | flops 589824 | bytes 4718592 | tf_op jit(solution)/shard_map/merge/pallas_call | solution.py:754
  266.0 9.4 %collective-permute-done.21 = bf16[4,48,1664]{2,1,0:T(8,128)(2,1)S(1)} collective-permute-done((bf16[4,48,1664]{2,1,0:T(8,128)(2,1)S(1)}, bf16[4,48,1664]{2,1,0:T(8,128)(2,1)S(1)}, u32[]{:S(2)}, u32[]{:S(2)}) %collective-permute-start.21) | collective-permute-done | bytes 639008 | tf_op jit(solution)/shard_map/ppermute | solution.py:803
  275.8 10.1 %collective-permute-done.22 = bf16[2,48,1664]{2,1,0:T(8,128)(2,1)S(1)} collective-permute-done((bf16[2,48,1664]{2,1,0:T(8,128)(2,1)S(1)}, bf16[2,48,1664]{2,1,0:T(8,128)(2,1)S(1)}, u32[]{:S(2)}, u32[]{:S(2)}) %collective-permute-start.22) | collective-permute-done | bytes 319520 | tf_op jit(solution)/shard_map/ppermute | solution.py:803
  286.1 4.1 %expert_grads.1 = (f32[768,768]{1,0:T(8,128)}, f32[768,768]{1,0:T(8,128)}) custom-call(bf16[256,768]{1,0:T(8,128)(2,1)} %get-tuple-element.90.slots_ref, bf16[256,768]{1,0:T(8,128)(2,1)} %get-tuple-element.91.grads_ref, bf16[256,768]{1,0:T(8,128)(2,1)} %get-tuple-element.92.hidden_ref, bf16[256,768]{1,0:T(8,128)(2,1)} %get-tuple-element.93.pre_ref), custom_call_target="tpu_custom_call" | custom-call | flops 603979776 | bytes 6291456 | tf_op jit(solution)/shard_map/expert_grads/pallas_call | solution.py:434
  290.3 7.6 %block_output.1 = bf16[1182,768]{1,0:T(8,128)(2,1)} custom-call(f32[6,208,768]{2,1,0:T(8,128)} %get-tuple-element.65.y_ref, f32[6,8,208]{2,1,0:T(8,128)} %get-tuple-element.66.logits_ref, bf16[128,768]{1,0:T(8,128)(2,1)} %bitcast.49), custom_call_target="tpu_custom_call" | custom-call | flops 398721024 | bytes 5750784 | tf_op jit(solution)/shard_map/block_output/pallas_call | solution.py:572
  (122 shorter events, 34.8 us)
Async XLA Ops:
  1.3 4.6 %collective-permute-start.1 = (bf16[2,192]{1,0:T(2,128)(2,1)S(1)}, bf16[2,192]{1,0:T(2,128)(2,1)S(1)}, u32[]{:S(2)}, u32[]{:S(2)}) collective-permute-start(bf16[2,192]{1,0:T(2,128)(2,1)S(1)} %fusion.11), channel_id=1, source_target_pairs={{0,2},{1,3},{2,0},{3,1},{4,6},{5,7},{6,4},{7,5},{8,10},{9,11},{10,... | collective-permute-start | bytes 2312 | tf_op jit(solution)/shard_map/ppermute | solution.py:770
  6.0 1.5 collective-permute-start.2
  7.0 1.5 collective-permute-start
  9.7 9.9 %collective-permute-start.3 = (bf16[1,48,1280]{2,1,0:T(8,128)(2,1)S(1)}, bf16[1,48,1280]{2,1,0:T(8,128)(2,1)S(1)}, u32[]{:S(2)}, u32[]{:S(2)}) collective-permute-start(bf16[1,48,1280]{2,1,0:T(8,128)(2,1)S(1)} %fusion.3), channel_id=1, source_target_pairs={{0,16},{1,5},{2,18},{3,7},{4,20},{5,1},{6,22},{7,3},{8,24},{9,13},... | collective-permute-start | bytes 368648 | tf_op jit(solution)/shard_map/ppermute | solution.py:840
  19.7 7.8 %collective-permute-start.4 = (bf16[2,48,1280]{2,1,0:T(8,128)(2,1)S(1)}, bf16[2,48,1280]{2,1,0:T(8,128)(2,1)S(1)}, u32[]{:S(2)}, u32[]{:S(2)}) collective-permute-start(bf16[2,48,1280]{2,1,0:T(8,128)(2,1)S(1)} %pad_maximum_fusion.4), channel_id=1, source_target_pairs={{0,8},{1,17},{2,10},{3,19},{4,12},{5,21},{6,14},{7,23},{8,0},{9,25... | collective-permute-start | bytes 737288 | tf_op jit(solution)/shard_map/ppermute | solution.py:840
  27.5 8.9 %collective-permute-start.5 = (bf16[4,48,1280]{2,1,0:T(8,128)(2,1)S(1)}, bf16[4,48,1280]{2,1,0:T(8,128)(2,1)S(1)}, u32[]{:S(2)}, u32[]{:S(2)}) collective-permute-start(bf16[4,48,1280]{2,1,0:T(8,128)(2,1)S(1)} %pad_maximum_fusion.2), channel_id=1, source_target_pairs={{0,4},{1,9},{2,6},{3,11},{4,0},{5,13},{6,2},{7,15},{8,12},{9,1},{1... | collective-permute-start | bytes 1474568 | tf_op jit(solution)/shard_map/ppermute | solution.py:840
  29.0 5.1 %collective-permute-start.6 = (bf16[48,1536]{1,0:T(8,128)(2,1)S(1)}, bf16[48,1536]{1,0:T(8,128)(2,1)S(1)}, u32[]{:S(2)}, u32[]{:S(2)}) collective-permute-start(bf16[48,1536]{1,0:T(8,128)(2,1)S(1)} %bitcast.51), channel_id=1, source_target_pairs={{0,2},{1,3},{2,0},{3,1},{4,6},{5,7},{6,4},{7,5},{8,10},{9,11},{10,... | collective-permute-start | bytes 442376 | tf_op jit(solution)/shard_map/ppermute | solution.py:770
  36.5 35.3 %copy-start.3 = (bf16[8,48,1280]{2,1,0:T(8,128)(2,1)}, bf16[8,48,1280]{2,1,0:T(8,128)(2,1)S(1)}, u32[]{:S(2)}) copy-start(bf16[8,48,1280]{2,1,0:T(8,128)(2,1)S(1)} %pad_maximum_fusion.refs_4_) | copy-start | bytes 2949124
  36.5 13.1 %collective-permute-start.8 = (bf16[1,48,1920]{2,1,0:T(8,128)(2,1)S(1)}, bf16[1,48,1920]{2,1,0:T(8,128)(2,1)S(1)}, u32[]{:S(2)}, u32[]{:S(2)}) collective-permute-start(bf16[1,48,1920]{2,1,0:T(8,128)(2,1)S(1)} %maximum_bitcast_fusion), channel_id=1, source_target_pairs={{0,16},{1,5},{2,18},{3,7},{4,20},{5,1},{6,22},{7,3},{8,24},{9,13},... | collective-permute-start | bytes 552968 | tf_op jit(solution)/shard_map/ppermute | solution.py:847
  49.7 9.3 %collective-permute-start.9 = (bf16[2,48,1920]{2,1,0:T(8,128)(2,1)S(1)}, bf16[2,48,1920]{2,1,0:T(8,128)(2,1)S(1)}, u32[]{:S(2)}, u32[]{:S(2)}) collective-permute-start(bf16[2,48,1920]{2,1,0:T(8,128)(2,1)S(1)} %pad_maximum_fusion.3), channel_id=1, source_target_pairs={{0,8},{1,17},{2,10},{3,19},{4,12},{5,21},{6,14},{7,23},{8,0},{9,25... | collective-permute-start | bytes 1105928 | tf_op jit(solution)/shard_map/ppermute | solution.py:847
  59.1 12.6 %collective-permute-start.10 = (bf16[4,48,1920]{2,1,0:T(8,128)(2,1)S(1)}, bf16[4,48,1920]{2,1,0:T(8,128)(2,1)S(1)}, u32[]{:S(2)}, u32[]{:S(2)}) collective-permute-start(bf16[4,48,1920]{2,1,0:T(8,128)(2,1)S(1)} %pad_maximum_fusion.1), channel_id=1, source_target_pairs={{0,4},{1,9},{2,6},{3,11},{4,0},{5,13},{6,2},{7,15},{8,12},{9,1},{1... | collective-permute-start | bytes 2211848 | tf_op jit(solution)/shard_map/ppermute | solution.py:847
  71.7 21.7 %copy-start.5 = (bf16[8,48,1920]{2,1,0:T(8,128)(2,1)}, bf16[8,48,1920]{2,1,0:T(8,128)(2,1)S(1)}, u32[]{:S(2)}) copy-start(bf16[8,48,1920]{2,1,0:T(8,128)(2,1)S(1)} %constant_dynamic-update-slice_fusion.refs_4_) | copy-start | bytes 4423684
  71.8 21.7 %collective-permute-start.11 = (bf16[8,48,1920]{2,1,0:T(8,128)(2,1)S(1)}, bf16[8,48,1920]{2,1,0:T(8,128)(2,1)}, u32[]{:S(2)}, u32[]{:S(2)}) collective-permute-start(bf16[8,48,1920]{2,1,0:T(8,128)(2,1)S(1)} %constant_dynamic-update-slice_fusion.refs_4_), channel_id=1, source_target_pairs={{0,1},{1,0},{2,3},{3,2},{4,5},{5,4},{6,7},{7,6},{8,9},{9,8},{10,11... | collective-permute-start | bytes 4423688 | tf_op jit(solution)/shard_map/ppermute | solution.py:770
  71.8 4.7 %collective-permute-start.7 = (bf16[8,48,1280]{2,1,0:T(8,128)(2,1)S(1)}, bf16[8,48,1280]{2,1,0:T(8,128)(2,1)S(1)}, u32[]{:S(2)}, u32[]{:S(2)}) collective-permute-start(bf16[8,48,1280]{2,1,0:T(8,128)(2,1)S(1)} %pad_maximum_fusion.refs_4_), channel_id=1, source_target_pairs={{0,1},{1,0},{2,3},{3,2},{4,5},{5,4},{6,7},{7,6},{8,9},{9,8},{10,11... | collective-permute-start | bytes 2949128 | tf_op jit(solution)/shard_map/ppermute | solution.py:770
  133.1 5.7 %collective-permute-start.12 = (bf16[8,16,768]{2,1,0:T(8,128)(2,1)S(1)}, bf16[8,16,768]{2,1,0:T(8,128)(2,1)S(1)}, u32[]{:S(2)}, u32[]{:S(2)}) collective-permute-start(bf16[8,16,768]{2,1,0:T(8,128)(2,1)S(1)} %all_to_all.10), channel_id=1, source_target_pairs={{0,2},{1,3},{2,0},{3,1},{4,6},{5,7},{6,4},{7,5},{8,10},{9,11},{10,... | collective-permute-start | bytes 589832 | tf_op jit(solution)/shard_map/ppermute | solution.py:770
  138.8 1.8 copy-start.4
  138.8 1.8 collective-permute-start.13
  145.8 1.9 collective-permute-start.14
  148.8 7.0 %collective-permute-start.15 = (bf16[8,16,768]{2,1,0:T(8,128)(2,1)S(1)}, bf16[8,16,768]{2,1,0:T(8,128)(2,1)S(1)}, u32[]{:S(2)}, u32[]{:S(2)}) collective-permute-start(bf16[8,16,768]{2,1,0:T(8,128)(2,1)S(1)} %slice.112), channel_id=1, source_target_pairs={{0,2},{1,3},{2,0},{3,1},{4,6},{5,7},{6,4},{7,5},{8,10},{9,11},{10,... | collective-permute-start | bytes 589832 | tf_op jit(solution)/shard_map/ppermute | solution.py:770
  204.0 3.1 %collective-permute-start.16 = (bf16[8,48,1536]{2,1,0:T(8,128)(2,1)}, bf16[8,48,1536]{2,1,0:T(8,128)(2,1)S(1)}, u32[]{:S(2)}, u32[]{:S(2)}) collective-permute-start(bf16[8,48,1536]{2,1,0:T(8,128)(2,1)} %get-tuple-element.78), channel_id=1, source_target_pairs={{0,1},{1,0},{2,3},{3,2},{4,5},{5,4},{6,7},{7,6},{8,9},{9,8},{10,11... | collective-permute-start | bytes 3538952 | tf_op jit(solution)/shard_map/ppermute | solution.py:770
  208.6 21.5 %copy-start.6 = (f32[16,768]{1,0:T(8,128)S(1)}, f32[16,768]{1,0:T(8,128)}, u32[]{:S(2)}) copy-start(f32[16,768]{1,0:T(8,128)} %get-tuple-element.89) | copy-start | bytes 147460
  228.3 30.2 %collective-permute-start.17 = (bf16[8,48,1536]{2,1,0:T(8,128)(2,1)}, bf16[8,48,1536]{2,1,0:T(8,128)(2,1)S(1)}, u32[]{:S(2)}, u32[]{:S(2)}) collective-permute-start(bf16[8,48,1536]{2,1,0:T(8,128)(2,1)} %get-tuple-element.86), channel_id=1, source_target_pairs={{0,1},{1,0},{2,3},{3,2},{4,5},{5,4},{6,7},{7,6},{8,9},{9,8},{10,11... | collective-permute-start | bytes 3538952 | tf_op jit(solution)/shard_map/ppermute | solution.py:770
  228.4 30.1 %collective-permute-start.18 = (bf16[8,48,1536]{2,1,0:T(8,128)(2,1)S(1)}, bf16[8,48,1536]{2,1,0:T(8,128)(2,1)S(1)}, u32[]{:S(2)}, u32[]{:S(2)}) collective-permute-start(bf16[8,48,1536]{2,1,0:T(8,128)(2,1)S(1)} %add_convert_fusion), channel_id=1, source_target_pairs={{0,2},{1,3},{2,0},{3,1},{4,6},{5,7},{6,4},{7,5},{8,10},{9,11},{10,... | collective-permute-start | bytes 3538952 | tf_op jit(solution)/shard_map/ppermute | solution.py:770
  251.0 1.3 collective-permute-start.19
  252.3 5.4 %collective-permute-start.20 = (f32[12,768]{1,0:T(8,128)S(1)}, f32[12,768]{1,0:T(8,128)S(1)}, u32[]{:S(2)}, u32[]{:S(2)}) collective-permute-start(f32[12,768]{1,0:T(8,128)S(1)} %fusion.13), channel_id=1, source_target_pairs={{0,2},{1,3},{2,0},{3,1},{4,6},{5,7},{6,4},{7,5},{8,10},{9,11},{10,... | collective-permute-start | bytes 110600 | tf_op jit(solution)/shard_map/ppermute | solution.py:770
  258.4 1.0 copy-start.1
  258.5 1.4 copy-start.2
  263.7 11.7 %copy-start = (bf16[8,48,1664]{2,1,0:T(8,128)(2,1)S(1)}, bf16[8,48,1664]{2,1,0:T(8,128)(2,1)}, u32[]{:S(2)}) copy-start(bf16[8,48,1664]{2,1,0:T(8,128)(2,1)} %merge.1) | copy-start | bytes 3833860
  264.9 10.5 %collective-permute-start.21 = (bf16[4,48,1664]{2,1,0:T(8,128)(2,1)S(1)}, bf16[4,48,1664]{2,1,0:T(8,128)(2,1)S(1)}, u32[]{:S(2)}, u32[]{:S(2)}) collective-permute-start(bf16[4,48,1664]{2,1,0:T(8,128)(2,1)S(1)} %slice.116), channel_id=1, source_target_pairs={{0,4},{1,9},{2,6},{3,11},{4,0},{5,13},{6,2},{7,15},{8,12},{9,1},{1... | collective-permute-start | bytes 1916936 | tf_op jit(solution)/shard_map/ppermute | solution.py:803
  275.6 10.4 %collective-permute-start.22 = (bf16[2,48,1664]{2,1,0:T(8,128)(2,1)S(1)}, bf16[2,48,1664]{2,1,0:T(8,128)(2,1)S(1)}, u32[]{:S(2)}, u32[]{:S(2)}) collective-permute-start(bf16[2,48,1664]{2,1,0:T(8,128)(2,1)S(1)} %slice.118), channel_id=1, source_target_pairs={{0,8},{1,17},{2,10},{3,19},{4,12},{5,21},{6,14},{7,23},{8,0},{9,25... | collective-permute-start | bytes 958472 | tf_op jit(solution)/shard_map/ppermute | solution.py:803
  286.1 11.8 %collective-permute-start.23 = (bf16[1,48,1664]{2,1,0:T(8,128)(2,1)S(1)}, bf16[1,48,1664]{2,1,0:T(8,128)(2,1)S(1)}, u32[]{:S(2)}, u32[]{:S(2)}) collective-permute-start(bf16[1,48,1664]{2,1,0:T(8,128)(2,1)S(1)} %slice.120), channel_id=1, source_target_pairs={{0,16},{1,5},{2,18},{3,7},{4,20},{5,1},{6,22},{7,3},{8,24},{9,13},... | collective-permute-start | bytes 479240 | tf_op jit(solution)/shard_map/ppermute | solution.py:803
  298.9 1.5 collective-permute-start.24
  (2 other events, 1.7 us)
